TPU v7x, 256 devices: a whole 4x4x8 slice. The times are simulated.
256 devices in a mesh: expert: 64 (over z, x, core), tensor: 4 (over y).
Axes of the slice: x: 4, y: 4, z: 8, core: 2. Of those that a mesh axis runs over, the one named last changes fastest.
Arguments:
- tokens: bfloat16 [8192, 3584], P('expert', 'tensor'), may hold values from -6 to 6
- tangents: bfloat16 [8192, 3584], P('expert', 'tensor'), may hold values from -6 to 6
- routes: int32 [8192, 8], P('expert'), may hold values from 0 to 63, all different within a row; in each aligned block of 128 rows (0 to 127, 128 to 255, ...) at most 20 rows name the same one
- gates: float32 [8192, 8], P('expert'), may hold values from 0.02 to 0.6
- gate_weight: bfloat16 [64, 3584, 1024], P('expert', None, 'tensor'), may hold values from -0.09375 to 0.09375
- up_weight: bfloat16 [64, 3584, 1024], P('expert', None, 'tensor'), may hold values from -0.09375 to 0.09375
- down_weight: bfloat16 [64, 1024, 3584], P('expert', 'tensor'), may hold values from -0.1875 to 0.1875
- readout: bfloat16 [3584], replicated, may hold values from -6 to 6
Outputs:
- curvature: bfloat16 [8192, 3584], P('expert', 'tensor')
Inputs may be any that keep to these rules, and one draw needn't show every extreme that they name: `routes`: A token's 8 experts differ. Among the tokens of one index of expert (aligned blocks of 128 tokens) no expert is named more than 20 times, a bound that some block reaches.
All inputs are finite; a program needn't handle non-finite values.
Results may differ from a plain program's by a relative error of at most 0.012.
Values may be sent and summed in bfloat16 or wider, within the bound.
A program may use at most 128 MiB of HBM per device.

v0:
```python
import jax
import jax.numpy as jnp
from jax import lax
from jax.sharding import PartitionSpec as P


def shards(tokens, tangents, routes, gates, gate_weight, up_weight, down_weight, readout):
    experts = lax.axis_size("expert")
    tok_rows = tokens.shape[0]
    top_count = routes.shape[1]
    slots = tok_rows * top_count
    most_rows = slots * 5 // (4 * experts)
    destination = routes.reshape(-1)
    one_hot = (destination[:, None] == jnp.arange(experts, dtype=jnp.int32)[None, :]).astype(
        jnp.int32
    )
    earlier = jnp.cumsum(one_hot, axis=0) - one_hot
    position = jnp.sum(earlier * one_hot, axis=1)
    source_row = jnp.arange(slots, dtype=jnp.int32) // top_count

    def packed(rows):
        buffer = jnp.zeros((experts, most_rows, rows.shape[1]), rows.dtype)
        return buffer.at[destination, position].set(rows[source_row])

    wide_x, wide_v = (
        lax.all_gather(tokens, "tensor", axis=1, tiled=True),
        lax.all_gather(tangents, "tensor", axis=1, tiled=True),
    )
    got_x, got_v = (
        lax.all_to_all(packed(wide_x), "expert", split_axis=0, concat_axis=0, tiled=True),
        lax.all_to_all(packed(wide_v), "expert", split_axis=0, concat_axis=0, tiled=True),
    )
    width = got_x.shape[2]
    rows_x = got_x.reshape(experts * most_rows, width)
    rows_v = got_v.reshape(experts * most_rows, width)
    w_gate = gate_weight[0]
    w_up = up_weight[0]
    back = jnp.dot(down_weight[0], readout, preferred_element_type=jnp.float32)
    h = jnp.dot(rows_x, w_gate, preferred_element_type=jnp.float32)
    u = jnp.dot(rows_x, w_up, preferred_element_type=jnp.float32)
    dh = jnp.dot(rows_v, w_gate, preferred_element_type=jnp.float32)
    du = jnp.dot(rows_v, w_up, preferred_element_type=jnp.float32)
    sig = jax.nn.sigmoid(h)
    first = sig * (1.0 + h * (1.0 - sig))
    second = sig * (1.0 - sig) * (2.0 + h * (1.0 - 2.0 * sig))
    coef_gate = (back[None, :] * (du * first + u * second * dh)).astype(jnp.bfloat16)
    coef_up = (back[None, :] * first * dh).astype(jnp.bfloat16)
    contract = (((1,), (1,)), ((), ()))
    partial_value = lax.dot_general(coef_gate, w_gate, contract, preferred_element_type=jnp.float32)
    partial_value = partial_value + lax.dot_general(
        coef_up, w_up, contract, preferred_element_type=jnp.float32
    )
    partial_value = partial_value.astype(jnp.bfloat16).reshape(experts, most_rows, width)
    returned = lax.all_to_all(partial_value, "expert", split_axis=0, concat_axis=0, tiled=True)
    picked = returned[destination, position]
    weighted = picked.astype(jnp.float32) * gates.reshape(-1)[:, None]
    per_token = jnp.sum(weighted.reshape(tok_rows, top_count, width), axis=1)
    result = lax.psum_scatter(per_token, "tensor", scatter_dimension=1, tiled=True)
    return result.astype(jnp.bfloat16)


def solution(mesh):
    return jax.shard_map(
        shards,
        mesh=mesh,
        in_specs=(
            P("expert", "tensor"),
            P("expert", "tensor"),
            P("expert", None),
            P("expert", None),
            P("expert", None, "tensor"),
            P("expert", None, "tensor"),
            P("expert", "tensor", None),
            P(),
        ),
        out_specs=P("expert", "tensor"),
        check_vma=False,
    )
```

profile of v0, /device:TPU:9, one launch (start us, length us, event | category | flops | bytes accessed | tf_op | source)
XLA Modules:
  0.0 1004.3 jit_solution(12254609463102750347)
XLA Ops:
  7.8 18.0 %reduce-window.6 = s32[64,8,128]{2,1,0:T(8,128)S(1)} reduce-window(s32[64,8,128]{2,1,0:T(8,128)S(1)} %fusion.39, s32[]{:T(128)} %constant.27.clone.1), window={size=1x1x128 pad=0_0x0_0x127_0}, to_apply=%region_0.0 | reduce-window | flops 8323072 | bytes 524292 | tf_op jit(solution)/shard_map/reduce-window
  26.7 12.5 %all_gather.7 = bf16[128,3584]{1,0:T(8,128)(2,1)S(1)} all-gather(bf16[128,896]{1,0:T(8,128)(2,1)S(1)} %copy-done.2), channel_id=1, replica_groups=mesh['expert'=64,'tensor'=4] {'tensor'}, dimensions={1}, use_global_device_ids=true | all-gather | bytes 1146880 | tf_op jit(solution)/shard_map/all_gather | solution.py:26
  39.2 37.8 %scatter_custom_fusion.1 = bf16[1280,3584]{1,0:T(8,128)(2,1)} fusion(s32[1024]{0:T(1024)S(1)} %get-tuple-element.9, bf16[128,3584]{1,0:T(8,128)(2,1)S(1)} %all_gather.7, s32[1024]{0:T(1024)S(1)} %get-tuple-element.8, bf16[]{:T(256)} %constant.26.clone.1), kind=kCustom, calls=%fused_computation.9 | custom fusion | bytes 9175042
  77.0 12.7 %copy.33 = bf16[64,20,3584]{2,1,0:T(8,128)(2,1)} copy(bf16[64,20,3584]{2,0,1:T(8,128)(2,1)} %bitcast.56) | data formatting | bytes 18350080 | tf_op jit(solution)/shard_map/scatter | solution.py:23
  89.8 15.0 %all-to-all-start.1 = ((bf16[64,20,3584]{2,1,0:T(8,128)(2,1)}), bf16[64,20,3584]{2,1,0:T(8,128)(2,1)}, u32[]{:S(2)}, u32[]{:S(2)}) async-start(bf16[64,20,3584]{2,1,0:T(8,128)(2,1)} %copy.33), calls=%async_computation.1 | async-start | bytes 22020096 | tf_op jit(solution)/shard_map/all_to_all | solution.py:30
  104.9 12.0 %all_gather.6 = bf16[128,3584]{1,0:T(8,128)(2,1)S(1)} all-gather(bf16[128,896]{1,0:T(8,128)(2,1)S(1)} %copy-done.3), channel_id=1, replica_groups=mesh['expert'=64,'tensor'=4] {'tensor'}, dimensions={1}, use_global_device_ids=true | all-gather | bytes 1146880 | tf_op jit(solution)/shard_map/all_gather | solution.py:27
  116.8 37.8 %scatter_custom_fusion = bf16[1280,3584]{1,0:T(8,128)(2,1)} fusion(s32[1024]{0:T(1024)S(1)} %get-tuple-element.9, bf16[128,3584]{1,0:T(8,128)(2,1)S(1)} %all_gather.6, s32[1024]{0:T(1024)S(1)} %get-tuple-element.8, bf16[]{:T(256)} %constant.26.clone.1), kind=kCustom, calls=%fused_computation.11 | custom fusion | bytes 9175042
  154.6 12.7 %copy.32 = bf16[64,20,3584]{2,1,0:T(8,128)(2,1)} copy(bf16[64,20,3584]{2,0,1:T(8,128)(2,1)} %bitcast.55) | data formatting | bytes 18350080 | tf_op jit(solution)/shard_map/scatter | solution.py:23
  167.3 176.9 %all-to-all-done.1 = bf16[64,20,3584]{2,1,0:T(8,128)(2,1)} async-done(((bf16[64,20,3584]{2,1,0:T(8,128)(2,1)}), bf16[64,20,3584]{2,1,0:T(8,128)(2,1)}, u32[]{:S(2)}, u32[]{:S(2)}) %all-to-all-start.1) | async-done | bytes 9175072 | tf_op jit(solution)/shard_map/all_to_all | solution.py:30
  344.3 11.9 %all-to-all-start = ((bf16[64,20,3584]{2,1,0:T(8,128)(2,1)}), bf16[64,20,3584]{2,1,0:T(8,128)(2,1)}, u32[]{:S(2)}, u32[]{:S(2)}) async-start(bf16[64,20,3584]{2,1,0:T(8,128)(2,1)} %copy.32), calls=%async_computation | async-start | bytes 22020096 | tf_op jit(solution)/shard_map/all_to_all | solution.py:31
  358.2 13.3 %reshape.127 = bf16[1280,3584]{1,0:T(8,128)(2,1)} reshape(bf16[64,20,3584]{2,1,0:T(8,128)(2,1)} %all-to-all-done.1) | data formatting | bytes 18350080 | tf_op jit(solution)/shard_map/reshape | solution.py:34
  371.5 6.7 fusion.16
  378.2 216.3 %all-to-all-done = bf16[64,20,3584]{2,1,0:T(8,128)(2,1)} async-done(((bf16[64,20,3584]{2,1,0:T(8,128)(2,1)}), bf16[64,20,3584]{2,1,0:T(8,128)(2,1)}, u32[]{:S(2)}, u32[]{:S(2)}) %all-to-all-start) | async-done | bytes 9175072 | tf_op jit(solution)/shard_map/all_to_all | solution.py:31
  594.5 13.2 %reshape.126 = bf16[1280,3584]{1,0:T(8,128)(2,1)} reshape(bf16[64,20,3584]{2,1,0:T(8,128)(2,1)} %all-to-all-done) | data formatting | bytes 18350080 | tf_op jit(solution)/shard_map/reshape | solution.py:35
  607.8 7.9 fusion.14
  619.5 17.0 %fusion.12 = f32[1280,3584]{1,0:T(8,128)} fusion(f32[1280,256]{1,0:T(8,128)} %convolution_multiply_fusion.1, f32[1280,256]{1,0:T(8,128)} %fusion.14, bf16[1280,3584]{1,0:T(8,128)(2,1)} %reshape.127, bf16[1,3584,256]{2,1,0:T(8,128)(2,1)} %param.12, bf16[1,3584,256]{2,1,0:T(8,128)(2,1)S(1)} %copy-done, f32[1280,256]{1,0:T(8,128)S(1)} %fusion.16, ...), kind=kOutput, calls=%fused_computation.21 | convolution fusion | flops 4702535680 | bytes 35128320 | tf_op jit(solution)/shard_map/dot_general | solution.py:49
  636.5 10.5 %fusion = bf16[1280,3584]{1,0:T(8,128)(2,1)} fusion(f32[1280,3584]{1,0:T(8,128)} %fusion.12, bf16[1,3584,256]{2,1,0:T(8,128)(2,1)S(1)} %copy-done, f32[1280,256]{1,0:T(8,128)} %fusion.14, f32[256]{0:T(256)S(1)} %bitcast.59, f32[1280,256]{1,0:T(8,128)S(1)} %fusion.16), kind=kOutput, calls=%fused_computation.6 | convolution fusion | flops 2361262080 | bytes 31982592 | tf_op jit(solution)/shard_map/dot_general | solution.py:50
  647.0 13.1 %reshape.128 = bf16[64,20,3584]{2,1,0:T(8,128)(2,1)} reshape(bf16[1280,3584]{1,0:T(8,128)(2,1)} %fusion) | data formatting | bytes 18350080 | tf_op jit(solution)/shard_map/reshape | solution.py:53
  660.2 12.5 %all-to-all-start.2 = ((bf16[64,20,3584]{2,1,0:T(8,128)(2,1)}), bf16[64,20,3584]{2,1,0:T(8,128)(2,1)}, u32[]{:S(2)}, u32[]{:S(2)}) async-start(bf16[64,20,3584]{2,1,0:T(8,128)(2,1)} %reshape.128), calls=%async_computation.2 | async-start | bytes 22020096 | tf_op jit(solution)/shard_map/all_to_all | solution.py:54
  672.8 239.3 %all-to-all-done.2 = bf16[64,20,3584]{2,1,0:T(8,128)(2,1)} async-done(((bf16[64,20,3584]{2,1,0:T(8,128)(2,1)}), bf16[64,20,3584]{2,1,0:T(8,128)(2,1)}, u32[]{:S(2)}, u32[]{:S(2)}) %all-to-all-start.2) | async-done | bytes 9175072 | tf_op jit(solution)/shard_map/all_to_all | solution.py:54
  912.1 10.4 %copy.34 = bf16[64,20,3584]{2,0,1:T(8,128)(2,1)} copy(bf16[64,20,3584]{2,1,0:T(8,128)(2,1)} %all-to-all-done.2) | data formatting | bytes 18350080 | tf_op jit(solution)/shard_map/all_to_all | solution.py:54
  922.5 31.2 %gather_fusion = bf16[1024,3584]{1,0:T(8,128)(2,1)} fusion(bf16[64,20,3584]{2,0,1:T(8,128)(2,1)} %copy.34, s32[1024]{0:T(1024)S(1)} %bitcast.54), kind=kCustom, calls=%fused_computation.2 | custom fusion | bytes 14688256 | tf_op jit(solution)/shard_map/gather | solution.py:55
  953.7 11.0 %fusion.1 = f32[128,3584]{1,0:T(8,128)} fusion(bf16[1024,3584]{1,0:T(8,128)(2,1)} %gather_fusion, f32[128,8]{1,0:T(8,128)S(1)} %copy.35), kind=kLoop, calls=%fused_computation.8 | loop fusion | flops 10551296 | bytes 9179136 | tf_op jit(solution)/shard_map/reduce_sum | solution.py:57
  964.8 30.8 %reduce-scatter.2.cloned.1.call-done = f32[128,896]{1,0:T(8,128)} async-done(((f32[128,3584]{1,0:T(8,128)}), f32[128,896]{1,0:T(8,128)}) %reduce-scatter.2.cloned.1.call-update) | async-done | bytes 458768 | tf_op jit(solution)/shard_map/reduce_scatter | solution.py:58
  (40 shorter events, 9.9 us)
Async XLA Ops:
  6.5 609.1 %copy-start = (bf16[1,3584,256]{2,1,0:T(8,128)(2,1)S(1)}, bf16[1,3584,256]{2,1,0:T(8,128)(2,1)}, u32[]{:S(2)}) copy-start(bf16[1,3584,256]{2,1,0:T(8,128)(2,1)} %param.13) | copy-start | bytes 5505028
  6.5 19.9 %copy-start.7 = (s32[2]{0:T(128)S(1)}, s32[2]{0:T(128)}, u32[]{:S(2)}) copy-start(s32[2]{0:T(128)} %constant.44) | copy-start | bytes 28
  6.5 20.0 %copy-start.6 = (s32[2]{0:T(128)S(1)}, s32[2]{0:T(128)}, u32[]{:S(2)}) copy-start(s32[2]{0:T(128)} %constant.41) | copy-start | bytes 28
  6.5 20.1 %copy-start.2 = (bf16[128,896]{1,0:T(8,128)(2,1)S(1)}, bf16[128,896]{1,0:T(8,128)(2,1)}, u32[]{:S(2)}) copy-start(bf16[128,896]{1,0:T(8,128)(2,1)} %param.8) | copy-start | bytes 688132
  89.8 15.1 %copy-start.3 = (bf16[128,896]{1,0:T(8,128)(2,1)S(1)}, bf16[128,896]{1,0:T(8,128)(2,1)}, u32[]{:S(2)}) copy-start(bf16[128,896]{1,0:T(8,128)(2,1)} %param.9) | copy-start | bytes 688132
  89.8 254.5 %all-to-all-start.1 = ((bf16[64,20,3584]{2,1,0:T(8,128)(2,1)}), bf16[64,20,3584]{2,1,0:T(8,128)(2,1)}, u32[]{:S(2)}, u32[]{:S(2)}) async-start(bf16[64,20,3584]{2,1,0:T(8,128)(2,1)} %copy.33), calls=%async_computation.1 | async-start | bytes 22020096 | tf_op jit(solution)/shard_map/all_to_all | solution.py:30
  167.3 188.8 %copy-start.4 = (bf16[3584]{0:T(1024)(128)(2,1)S(1)}, bf16[3584]{0:T(1024)(128)(2,1)}, u32[]{:S(2)}) copy-start(bf16[3584]{0:T(1024)(128)(2,1)} %param.15) | copy-start | bytes 21508
  344.3 250.3 %all-to-all-start = ((bf16[64,20,3584]{2,1,0:T(8,128)(2,1)}), bf16[64,20,3584]{2,1,0:T(8,128)(2,1)}, u32[]{:S(2)}, u32[]{:S(2)}) async-start(bf16[64,20,3584]{2,1,0:T(8,128)(2,1)} %copy.32), calls=%async_computation | async-start | bytes 22020096 | tf_op jit(solution)/shard_map/all_to_all | solution.py:31
  607.8 7.9 copy-start.1
  660.2 12.5 %copy-start.5 = (f32[128,8]{0,1:T(8,128)S(1)}, f32[128,8]{0,1:T(8,128)}, u32[]{:S(2)}) copy-start(f32[128,8]{0,1:T(8,128)} %param.11) | copy-start | bytes 12292
  660.2 251.9 %all-to-all-start.2 = ((bf16[64,20,3584]{2,1,0:T(8,128)(2,1)}), bf16[64,20,3584]{2,1,0:T(8,128)(2,1)}, u32[]{:S(2)}, u32[]{:S(2)}) async-start(bf16[64,20,3584]{2,1,0:T(8,128)(2,1)} %reshape.128), calls=%async_computation.2 | async-start | bytes 22020096 | tf_op jit(solution)/shard_map/all_to_all | solution.py:54
  672.7 322.9 %reduce-scatter.2.cloned.1.call-start = ((), (), s32[]{:S(2)}) async-start(), calls=%async_computation.4 | async-start | bytes 2293760 | tf_op jit(solution)/shard_map/reduce_scatter | solution.py:58
Sparse Core Ops, SparseCore 0:
  964.9 30.5 reduce-scatter.1
where the time goes:
time: 1010 us; the launch traced here: 1000 us
  waiting for transfers between devices  663 us (66%)
  local copies, waits for them, and re-layouts  184 us (18%)
  matrix products  48 us (5%)
  starting transfers between devices  39.4 us (4%)
  other arithmetic  31.2 us (3%)
  blocking collectives  24.5 us (2%)
  between operations  13.8 us (1%)
    all_to_all x1, waiting for transfers between devices, shards(): lax.all_to_all(partial_value, 'expert', split_axis=0, concat_axis=0, tile...  239 us
    all_to_all x1, waiting for transfers between devices, shards(): lax.all_to_all(packed(wide_v), 'expert', split_axis=0, concat_axis=0, til...  216 us
    all_to_all x1, waiting for transfers between devices, shards(): lax.all_to_all(packed(wide_x), 'expert', split_axis=0, concat_axis=0, til...  177 us
    unnamed x21, local copies, waits for them, and re-layouts  76.7 us
    gather x1, local copies, waits for them, and re-layouts, shards(): picked = returned[destination, position]  31.2 us
    reduce_scatter x1, waiting for transfers between devices, shards(): lax.psum_scatter(per_token, 'tensor', scatter_dimension=1, tiled=True)  30.8 us
    scatter x2, local copies, waits for them, and re-layouts, packed(): return buffer.at[destination, position].set(rows[source_row])  25.5 us
  transfers between devices with their start and end apart: 4, of which 4 were waited for; matrix products, arithmetic and copies ran while one was open for 7% of the time, Pallas kernels for 0%

commit v1 on v0

v1 whole, which is shorter than its diff:
```python
import jax
import jax.numpy as jnp
from jax import lax
from jax.sharding import PartitionSpec as P


def shards(tokens, tangents, routes, gates, gate_weight, up_weight, down_weight, readout):
    experts = lax.axis_size("expert")
    parts = lax.axis_size("tensor")
    tok_rows, top_count = routes.shape
    most = tok_rows * top_count * 5 // (4 * experts)
    share = most // parts
    mine = lax.axis_index("tensor")

    named = routes[:, :, None] == jnp.arange(experts, dtype=jnp.int32)[None, None, :]
    chosen = jnp.any(named, axis=1)
    gate_of = jnp.sum(jnp.where(named, gates[:, :, None], 0.0), axis=1)
    before = jnp.tril(jnp.ones((tok_rows, tok_rows), jnp.bfloat16), -1)
    position = jnp.dot(before, chosen.astype(jnp.bfloat16), preferred_element_type=jnp.float32)
    position = jnp.where(chosen, position.astype(jnp.int32), -1)
    places = jnp.arange(share, dtype=jnp.int32) * parts + mine
    here = position[:, :, None] == places[None, None, :]
    select = here.reshape(tok_rows, experts * share)
    weight = jnp.where(here, gate_of[:, :, None], 0.0).reshape(tok_rows, experts * share)

    w_gate = lax.all_gather(gate_weight[0], "tensor", axis=0)
    w_up = lax.all_gather(up_weight[0], "tensor", axis=0)
    back = jnp.dot(down_weight[0], readout, preferred_element_type=jnp.float32)
    back = lax.all_gather(back, "tensor", axis=0)

    wide = lax.all_gather(jnp.stack([tokens, tangents], 0), "tensor", axis=2, tiled=True)
    width = wide.shape[2]
    pick = select.astype(jnp.bfloat16)
    rows_of = (((0,), (0,)), ((), ()))
    send = jnp.concatenate(
        [lax.dot_general(pick, wide[i], rows_of, preferred_element_type=jnp.float32) for i in (0, 1)], 1
    ).astype(jnp.bfloat16)
    got = lax.all_to_all(send, "expert", split_axis=0, concat_axis=0, tiled=True)
    rows_x, rows_v = got[:, :width], got[:, width:]

    total = jnp.zeros((experts * share, width), jnp.float32)
    contract = (((1,), (1,)), ((), ()))
    for b in range(parts):
        h = jnp.dot(rows_x, w_gate[b], preferred_element_type=jnp.float32)
        u = jnp.dot(rows_x, w_up[b], preferred_element_type=jnp.float32)
        dh = jnp.dot(rows_v, w_gate[b], preferred_element_type=jnp.float32)
        du = jnp.dot(rows_v, w_up[b], preferred_element_type=jnp.float32)
        sig = jax.nn.sigmoid(h)
        first = sig * (1.0 + h * (1.0 - sig))
        second = sig * (1.0 - sig) * (2.0 + h * (1.0 - 2.0 * sig))
        coef_gate = (back[b][None, :] * (du * first + u * second * dh)).astype(jnp.bfloat16)
        coef_up = (back[b][None, :] * first * dh).astype(jnp.bfloat16)
        total = total + lax.dot_general(coef_gate, w_gate[b], contract, preferred_element_type=jnp.float32)
        total = total + lax.dot_general(coef_up, w_up[b], contract, preferred_element_type=jnp.float32)
    returned = lax.all_to_all(total.astype(jnp.bfloat16), "expert", split_axis=0, concat_axis=0, tiled=True)
    high = weight.astype(jnp.bfloat16)
    low = (weight - high.astype(jnp.float32)).astype(jnp.bfloat16)
    per_token = jnp.dot(high, returned, preferred_element_type=jnp.float32) + jnp.dot(
        low, returned, preferred_element_type=jnp.float32
    )
    result = lax.psum_scatter(per_token, "tensor", scatter_dimension=1, tiled=True)
    return result.astype(jnp.bfloat16)


def solution(mesh):
    return jax.shard_map(
        shards,
        mesh=mesh,
        in_specs=(
            P("expert", "tensor"),
            P("expert", "tensor"),
            P("expert", None),
            P("expert", None),
            P("expert", None, "tensor"),
            P("expert", None, "tensor"),
            P("expert", "tensor", None),
            P(),
        ),
        out_specs=P("expert", "tensor"),
        check_vma=False,
    )
```

time: 1010 us -> 455 us (0.45)
  waiting for transfers between devices: 663 us -> 294 us
  local copies, waits for them, and re-layouts: 184 us -> 20.2 us
  matrix products: 48 us -> 90.8 us
  other arithmetic: 31.2 us -> 5.22 us
  starting transfers between devices: 39.4 us -> 20.7 us
  blocking collectives: 24.5 us -> 7.35 us
    all_to_all x3 -> x2, waiting for transfers between devices: 633 us -> 235 us  [the longest x1 152 us: shards(): lax.all_to_all(send, 'expert', split_axis=0, concat_axis=0, tiled=True)]
    unnamed x21 -> x19, local copies, waits for them, and re-layouts: 76.7 us -> 1.69 us
    dot_general x5 -> x25, matrix products: 46 us -> 90.3 us  [the longest x4 34.1 us: shards(): lax.dot_general(coef_gate, w_gate[b], contract, preferred_element_type=jn...]
    reshape x4 -> x0, local copies, waits for them, and re-layouts: 39.7 us -> none  [the longest x1 13.3 us: shards(): rows_x = got_x.reshape(experts * most_rows, width)]
    all_gather x0 -> x3, waiting for transfers between devices: none -> 31.7 us  [the longest x1 31.7 us: shards(): lax.all_gather(jnp.stack([tokens, tangents], 0), 'tensor', axis=2, tiled=...]
    gather x1 -> x0, local copies, waits for them, and re-layouts: 31.2 us -> none  [shards(): picked = returned[destination, position]]
    scatter x2 -> x0, local copies, waits for them, and re-layouts: 25.5 us -> none  [packed(): return buffer.at[destination, position].set(rows[source_row])]
    all_to_all x3 -> x2, starting transfers between devices: 39.4 us -> 20.6 us  [the longest x1 11 us: shards(): lax.all_to_all(send, 'expert', split_axis=0, concat_axis=0, tiled=True)]
  transfers between devices with their start and end apart: 4 -> 6, of which waited for: 4 -> 4; matrix products, arithmetic and copies ran while one was open for 7% -> 5% of each run, Pallas kernels for 0% -> 0%
where the time goes in v1:
time: 455 us; the launch traced here: 452 us
  waiting for transfers between devices  294 us (65%)
  matrix products  90.8 us (20%)
  starting transfers between devices  20.7 us (5%)
  local copies, waits for them, and re-layouts  20.2 us (4%)
  between operations  13.4 us (3%)
  blocking collectives  7.35 us (2%)
  other arithmetic  5.22 us (1%)
    all_to_all x1, waiting for transfers between devices, shards(): lax.all_to_all(send, 'expert', split_axis=0, concat_axis=0, tiled=True)  152 us
    all_to_all x1, waiting for transfers between devices, shards(): lax.all_to_all(total.astype(jnp.bfloat16), 'expert', split_axis=0, concat...  83.6 us
    dot_general x4, matrix products, shards(): lax.dot_general(coef_gate, w_gate[b], contract, preferred_element_type=jn...  34.1 us
    all_gather x1, waiting for transfers between devices, shards(): lax.all_gather(jnp.stack([tokens, tangents], 0), 'tensor', axis=2, tiled=...  31.7 us
    reduce_scatter x1, waiting for transfers between devices, shards(): lax.psum_scatter(per_token, 'tensor', scatter_dimension=1, tiled=True)  26 us
    dot_general x4, matrix products, shards(): lax.dot_general(coef_up, w_up[b], contract, preferred_element_type=jnp.fl...  22.6 us
    dot_general x4, matrix products, shards(): du = jnp.dot(rows_v, w_up[b], preferred_element_type=jnp.float32)  11.8 us
    all_to_all x1, starting transfers between devices, shards(): lax.all_to_all(send, 'expert', split_axis=0, concat_axis=0, tiled=True)  11 us
  transfers between devices with their start and end apart: 6, of which 4 were waited for; matrix products, arithmetic and copies ran while one was open for 5% of the time, Pallas kernels for 0%

profile of v1, /device:TPU:9, one launch (start us, length us, event | category | flops | bytes accessed | tf_op | source)
XLA Modules:
  0.0 452.0 jit_solution(5414016574919742583)
XLA Ops:
  10.7 31.7 %all-gather.6.cloned.1.call-done = bf16[2,128,3584]{2,1,0:T(8,128)(2,1)} async-done(((bf16[2,128,896]{2,1,0:T(8,128)(2,1)}), bf16[2,128,3584]{2,1,0:T(8,128)(2,1)}) %all-gather.6.cloned.1.call-update) | async-done | bytes 1835024 | tf_op jit(solution)/shard_map/all_gather | solution.py:31
  46.8 5.6 %copy.39 = bf16[64,5,7168]{2,1,0:T(8,128)(2,1)} copy(bf16[64,5,7168]{2,0,1:T(8,128)(2,1)S(1)} %pad_maximum_fusion) | data formatting | bytes 9175040 | tf_op jit(solution)/shard_map/concatenate | solution.py:35
  52.4 11.0 %all-to-all-start = ((bf16[64,5,7168]{2,1,0:T(8,128)(2,1)}), bf16[64,5,7168]{2,1,0:T(8,128)(2,1)}, u32[]{:S(2)}, u32[]{:S(2)}) async-start(bf16[64,5,7168]{2,1,0:T(8,128)(2,1)} %copy.39), calls=%async_computation | async-start | bytes 14680064 | tf_op jit(solution)/shard_map/all_to_all | solution.py:38
  64.6 7.3 %all-gather.1 = f32[4,1,256]{2,1,0:T(1,128)S(1)} all-gather(f32[1,1,256]{2,1,0:T(1,128)S(1)} %fusion.48), channel_id=2, replica_groups=mesh['expert'=64,'tensor'=4] {'tensor'}, dimensions={0}, use_global_device_ids=true | all-gather | bytes 5120 | tf_op jit(solution)/shard_map/all_gather | solution.py:29
  72.0 151.6 %all-to-all-done = bf16[64,5,7168]{2,1,0:T(8,128)(2,1)} async-done(((bf16[64,5,7168]{2,1,0:T(8,128)(2,1)}), bf16[64,5,7168]{2,1,0:T(8,128)(2,1)}, u32[]{:S(2)}, u32[]{:S(2)}) %all-to-all-start) | async-done | bytes 4587552 | tf_op jit(solution)/shard_map/all_to_all | solution.py:38
  223.6 8.2 %all_to_all.13 = bf16[320,7168]{1,0:T(8,128)(2,1)} reshape(bf16[64,5,7168]{2,1,0:T(8,128)(2,1)} %all-to-all-done) | data formatting | bytes 9175040 | tf_op jit(solution)/shard_map/all_to_all | solution.py:38
  231.8 3.1 fusion.8
  243.6 3.7 fusion.29
  247.3 7.6 %fusion.6 = f32[320,3584]{1,0:T(8,128)} fusion(bf16[4,3584,256]{2,1,0:T(8,128)(2,1)} %all-gather.10.cloned.1.call-done, f32[320,256]{1,0:T(8,128)} %fusion.29, f32[320,256]{1,0:T(8,128)S(1)} %fusion.7, bf16[4,3584,256]{2,1,0:T(8,128)(2,1)} %all-gather.8.cloned.1.call-done, bf16[320,7168]{1,0:T(8,128)(2,1)} %all_to_all.13, f32[320,256]{1,0:T(8,128)S(1)} %fusion.8, ...), kind=kOutput, calls=%fused_computation.26 | convolution fusion | flops 1175633920 | bytes 11535360 | tf_op jit(solution)/shard_map/dot_general | solution.py:53
  254.9 5.9 %convolution_add_fusion.6 = f32[320,3584]{1,0:T(8,128)} fusion(f32[320,3584]{1,0:T(8,128)} %fusion.6, bf16[4,3584,256]{2,1,0:T(8,128)(2,1)} %all-gather.8.cloned.1.call-done, f32[320,256]{1,0:T(8,128)S(1)} %fusion.7, f32[256]{0:T(256)S(1)} %bitcast.142, f32[320,256]{1,0:T(8,128)S(1)} %fusion.8), kind=kOutput, calls=%fused_computation.6 | convolution fusion | flops 589168640 | bytes 11666432 | tf_op jit(solution)/shard_map/dot_general | solution.py:54
  263.1 8.8 %convolution_add_fusion.5 = f32[320,3584]{1,0:T(8,128)} fusion(f32[320,3584]{1,0:T(8,128)} %convolution_add_fusion.6, bf16[4,3584,256]{2,1,0:T(8,128)(2,1)} %all-gather.10.cloned.1.call-done, f32[320,256]{1,0:T(8,128)S(1)} %fusion.27, f32[320,256]{1,0:T(8,128)S(1)} %fusion.11, bf16[4,3584,256]{2,1,0:T(8,128)(2,1)} %all-gather.8.cloned.1.call-done, ...), kind=kOutput, calls=%fused_computation.5 | convolution fusion | flops 1176780800 | bytes 16122880 | tf_op jit(solution)/shard_map/dot_general | solution.py:53
  271.9 5.8 %convolution_add_fusion.4 = f32[320,3584]{1,0:T(8,128)} fusion(f32[320,3584]{1,0:T(8,128)} %convolution_add_fusion.5, bf16[4,3584,256]{2,1,0:T(8,128)(2,1)} %all-gather.8.cloned.1.call-done, f32[320,256]{1,0:T(8,128)S(1)} %fusion.11, f32[256]{0:T(256)S(1)} %bitcast.140, f32[320,256]{1,0:T(8,128)S(1)} %fusion.12), kind=kOutput, calls=%fused_computation.4 | convolution fusion | flops 589168640 | bytes 11666432 | tf_op jit(solution)/shard_map/dot_general | solution.py:54
  277.6 2.9 fusion.25
  280.6 9.0 %convolution_add_fusion.3 = f32[320,3584]{1,0:T(8,128)} fusion(f32[320,3584]{1,0:T(8,128)} %convolution_add_fusion.4, bf16[4,3584,256]{2,1,0:T(8,128)(2,1)} %all-gather.10.cloned.1.call-done, f32[320,256]{1,0:T(8,128)S(1)} %fusion.25, f32[320,256]{1,0:T(8,128)S(1)} %fusion.15, bf16[4,3584,256]{2,1,0:T(8,128)(2,1)} %all-gather.8.cloned.1.call-done, ...), kind=kOutput, calls=%fused_computation.3 | convolution fusion | flops 1176780800 | bytes 16122880 | tf_op jit(solution)/shard_map/dot_general | solution.py:53
  289.6 5.8 %convolution_add_fusion.2 = f32[320,3584]{1,0:T(8,128)} fusion(f32[320,3584]{1,0:T(8,128)} %convolution_add_fusion.3, bf16[4,3584,256]{2,1,0:T(8,128)(2,1)} %all-gather.8.cloned.1.call-done, f32[320,256]{1,0:T(8,128)S(1)} %fusion.15, f32[256]{0:T(256)S(1)} %bitcast.138, f32[320,256]{1,0:T(8,128)S(1)} %fusion.16), kind=kOutput, calls=%fused_computation.2 | convolution fusion | flops 589168640 | bytes 11666432 | tf_op jit(solution)/shard_map/dot_general | solution.py:54
  295.4 2.9 fusion.23
  298.3 8.8 %convolution_add_fusion.1 = f32[320,3584]{1,0:T(8,128)} fusion(f32[320,3584]{1,0:T(8,128)} %convolution_add_fusion.2, bf16[4,3584,256]{2,1,0:T(8,128)(2,1)} %all-gather.10.cloned.1.call-done, f32[320,256]{1,0:T(8,128)S(1)} %fusion.23, f32[320,256]{1,0:T(8,128)S(1)} %fusion.19, bf16[4,3584,256]{2,1,0:T(8,128)(2,1)} %all-gather.8.cloned.1.call-done, ...), kind=kOutput, calls=%fused_computation.1 | convolution fusion | flops 1176780800 | bytes 16122880 | tf_op jit(solution)/shard_map/dot_general | solution.py:53
  307.1 5.1 %fusion = bf16[320,3584]{1,0:T(8,128)(2,1)} fusion(f32[320,3584]{1,0:T(8,128)} %convolution_add_fusion.1, bf16[4,3584,256]{2,1,0:T(8,128)(2,1)} %all-gather.8.cloned.1.call-done, f32[320,256]{1,0:T(8,128)S(1)} %fusion.19, f32[256]{0:T(256)S(1)} %bitcast.136, f32[320,256]{1,0:T(8,128)S(1)} %fusion.20), kind=kOutput, calls=%fused_computation.7 | convolution fusion | flops 590315520 | bytes 9372672 | tf_op jit(solution)/shard_map/dot_general | solution.py:54
  312.2 4.5 all_to_all.14
  316.7 9.6 %all-to-all-start.1 = ((bf16[64,5,3584]{2,1,0:T(8,128)(2,1)}), bf16[64,5,3584]{2,1,0:T(8,128)(2,1)}, u32[]{:S(2)}, u32[]{:S(2)}) async-start(bf16[64,5,3584]{2,1,0:T(8,128)(2,1)} %all_to_all.14), calls=%async_computation.1 | async-start | bytes 7340032 | tf_op jit(solution)/shard_map/all_to_all | solution.py:55
  326.4 83.6 %all-to-all-done.1 = bf16[64,5,3584]{2,1,0:T(8,128)(2,1)} async-done(((bf16[64,5,3584]{2,1,0:T(8,128)(2,1)}), bf16[64,5,3584]{2,1,0:T(8,128)(2,1)}, u32[]{:S(2)}, u32[]{:S(2)}) %all-to-all-start.1) | async-done | bytes 2293792 | tf_op jit(solution)/shard_map/all_to_all | solution.py:55
  410.0 3.3 convolution_bitcast_fusion
  413.3 4.4 fusion.1
  417.7 26.0 %reduce-scatter.2.cloned.1.call-done = f32[128,896]{1,0:T(8,128)} async-done(((f32[128,3584]{1,0:T(8,128)}), f32[128,896]{1,0:T(8,128)}) %reduce-scatter.2.cloned.1.call-update) | async-done | bytes 458768 | tf_op jit(solution)/shard_map/reduce_scatter | solution.py:61
  (56 shorter events, 22.5 us)
Async XLA Ops:
  6.5 57.5 %copy-start = (bf16[1,256,3584]{2,1,0:T(8,128)(2,1)S(1)}, bf16[1,256,3584]{2,1,0:T(8,128)(2,1)}, u32[]{:S(2)}) copy-start(bf16[1,256,3584]{2,1,0:T(8,128)(2,1)} %param.14) | copy-start | bytes 5505028
  6.5 35.8 %all-gather.6.cloned.1.call-start = ((), (), s32[]{:S(2)}) async-start(), calls=%async_computation.3 | async-start | bytes 2293760 | tf_op jit(solution)/shard_map/all_gather | solution.py:31
  8.6 223.3 %all-gather.10.cloned.1.call-start = ((), (), s32[]{:S(2)}) async-start(), calls=%async_computation.5 | async-start | bytes 9175040 | tf_op jit(solution)/shard_map/all_gather | solution.py:26
  52.3 11.7 %copy-start.5 = (bf16[3584]{0:T(1024)(128)(2,1)S(1)}, bf16[3584]{0:T(1024)(128)(2,1)}, u32[]{:S(2)}) copy-start(bf16[3584]{0:T(1024)(128)(2,1)} %param.15) | copy-start | bytes 21508
  52.4 171.3 %all-to-all-start = ((bf16[64,5,7168]{2,1,0:T(8,128)(2,1)}), bf16[64,5,7168]{2,1,0:T(8,128)(2,1)}, u32[]{:S(2)}, u32[]{:S(2)}) async-start(bf16[64,5,7168]{2,1,0:T(8,128)(2,1)} %copy.39), calls=%async_computation | async-start | bytes 14680064 | tf_op jit(solution)/shard_map/all_to_all | solution.py:38
  63.3 180.3 %all-gather.8.cloned.1.call-start = ((), (), s32[]{:S(2)}) async-start(), calls=%async_computation.4 | async-start | bytes 9175040 | tf_op jit(solution)/shard_map/all_gather | solution.py:27
  231.8 3.5 copy-start.2
  235.4 3.6 copy-start.3
  247.3 13.5 %slice-start = ((s8[4587520]{0:T(1024)(128)(4,1)}), s8[393216]{0:T(1024)(128)(4,1)S(1)}, s32[]{:S(2)}) async-start(s8[4587520]{0:T(1024)(128)(4,1)} %bitcast.131), calls=%async_computation.7 | async-start | bytes 786432
  254.9 5.9 %slice-start.1 = ((s8[4587520]{0:T(1024)(128)(4,1)}), s8[4194304]{0:T(1024)(128)(4,1)S(1)}, s32[]{:S(2)}) async-start(s8[4587520]{0:T(1024)(128)(4,1)} %bitcast.131), calls=%async_computation.8 | async-start | bytes 8388608
  316.7 9.7 %copy-start.4 = (s32[128,8]{0,1:T(8,128)S(1)}, s32[128,8]{0,1:T(8,128)}, u32[]{:S(2)}) copy-start(s32[128,8]{0,1:T(8,128)} %param.10) | copy-start | bytes 12292
  316.7 9.7 %copy-start.6 = (f32[128,8]{0,1:T(8,128)S(1)}, f32[128,8]{0,1:T(8,128)}, u32[]{:S(2)}) copy-start(f32[128,8]{0,1:T(8,128)} %param.11) | copy-start | bytes 12292
  316.7 93.4 %all-to-all-start.1 = ((bf16[64,5,3584]{2,1,0:T(8,128)(2,1)}), bf16[64,5,3584]{2,1,0:T(8,128)(2,1)}, u32[]{:S(2)}, u32[]{:S(2)}) async-start(bf16[64,5,3584]{2,1,0:T(8,128)(2,1)} %all_to_all.14), calls=%async_computation.1 | async-start | bytes 7340032 | tf_op jit(solution)/shard_map/all_to_all | solution.py:55
  326.3 117.4 %reduce-scatter.2.cloned.1.call-start = ((), (), s32[]{:S(2)}) async-start(), calls=%async_computation.6 | async-start | bytes 2293760 | tf_op jit(solution)/shard_map/reduce_scatter | solution.py:61
  410.0 35.4 %copy-start.1 = (bf16[1,256,3584]{2,1,0:T(8,128)(2,1)S(1)}, bf16[1,256,3584]{2,1,0:T(8,128)(2,1)}, u32[]{:S(2)}) copy-start(bf16[1,256,3584]{2,1,0:T(8,128)(2,1)} %param.14) | copy-start | bytes 5505028
Sparse Core Ops, SparseCore 0:
  9.2 33.0 all-gather.5
  44.1 77.8 all-gather.9
  123.8 77.7 all-gather.7
  417.8 25.8 reduce-scatter.1

commit v2 on v1

v2 whole, which is shorter than its diff:
```python
import functools

import jax
import jax.numpy as jnp
import numpy as np
from jax import lax
from jax.experimental import pallas as pl
from jax.experimental.pallas import tpu as pltpu
from jax.sharding import PartitionSpec as P

MESH = pl.DeviceIdType.MESH
NEAR = 8
F32 = jnp.float32
BF16 = jnp.bfloat16
NT = (((1,), (1,)), ((), ()))


def tables(nz, nd, share, parts):
    rows = nz * nd * 2 * share
    experts = nz * nd
    expand = np.zeros((rows, experts), np.float32)
    target = np.full((rows, 2), -100.0, np.float32)
    perm_out = np.zeros((rows, rows), np.float32)
    perm_back = np.zeros((rows, rows), np.float32)
    expand_back = np.zeros((experts, rows), np.float32)
    target_back = np.full((8, rows), -100.0, np.float32)
    for z in range(nz):
        for d in range(nd):
            for k in range(2):
                for q in range(share):
                    a = ((d * nz + z) * 2 + k) * share + q
                    b = ((z * 2 + k) * nd + d) * share + q
                    c = ((d * 2 + k) * nz + z) * share + q
                    e = z * nd + d
                    expand[a, e] = 1
                    target[a, k] = parts * q
                    perm_out[b, a] = 1
                    perm_back[c, b] = 1
                    expand_back[e, c] = 1
                    target_back[k, c] = parts * q
    return expand, target, perm_out, perm_back, expand_back, target_back


def kernel(
    dims,
    tok_ref, tan_ref, gw_ref, uw_ref, dw_ref,
    routes_ref, routes_t_ref, gates_ref, readout_ref,
    expand_ref, target_ref, perm_out_ref, perm_back_ref, expand_back_ref, target_back_ref,
    out_ref,
    T, S1, R1, S2, R2, W, H, C, acc, Q1, Q2, DW, BK, PTF, PTB, RS, P1, CB,
    local_sem, t_send, t_recv, w_send, w_recv, b_send, b_recv,
    s1_send, s1_recv, s2_send, s2_recv, q1_send, q1_recv, q2_send, q2_recv, r_send, r_recv,
):
    nz, nd, share, parts = dims
    toks, qw = tok_ref.shape
    depth, ff = gw_ref.shape[1:]
    half_depth = depth // 2
    experts = nz * nd
    m1, m2 = nz * 2 * share, nd * 2 * share
    group = nd * share
    me, y = lax.axis_index("expert"), lax.axis_index("tensor")
    z, d = me // nd, lax.rem(me, nd)
    up_y, down_y, far_y = lax.rem(y + 1, parts), lax.rem(y + parts - 1, parts), lax.rem(y + 2, parts)

    def near(dd):
        return (z * nd + dd, y)

    def along(zz):
        return (zz * nd + d, y)

    def across(yy):
        return (me, yy)

    def rows_at(i, n):
        return pl.ds(pl.multiple_of(i * n, n), n)

    def remote(src, dst, ss, rs, dev):
        return pltpu.make_async_remote_copy(
            src_ref=src, dst_ref=dst, send_sem=ss, recv_sem=rs, device_id=dev, device_id_type=MESH
        )

    barrier = pltpu.get_barrier_semaphore()
    for yy in (up_y, down_y, far_y):
        pl.semaphore_signal(barrier, inc=1, device_id=across(yy), device_id_type=MESH)

    @pl.loop(1, nd)
    def _(k):
        pl.semaphore_signal(barrier, inc=1, device_id=near(lax.rem(d + k, nd)), device_id_type=MESH)

    @pl.loop(1, nz)
    def _(k):
        pl.semaphore_signal(barrier, inc=1, device_id=along(lax.rem(z + k, nz)), device_id_type=MESH)

    local = [
        pltpu.make_async_copy(tok_ref, T.at[0, pl.ds(0, toks)], local_sem.at[0]),
        pltpu.make_async_copy(tan_ref, T.at[0, pl.ds(toks, toks)], local_sem.at[1]),
        pltpu.make_async_copy(dw_ref.at[0], DW, local_sem.at[2]),
        pltpu.make_async_copy(gw_ref.at[0], W.at[0, :, pl.ds(0, ff)], local_sem.at[3]),
        pltpu.make_async_copy(uw_ref.at[0], W.at[0, :, pl.ds(ff, ff)], local_sem.at[4]),
    ]
    for c in local:
        c.start()
    pl.semaphore_wait(barrier, 3 + nd - 1 + nz - 1)

    def t_own(slot, kind, to):
        return remote(
            (tok_ref, tan_ref)[kind], T.at[slot, pl.ds(kind * toks, toks)],
            t_send.at[slot, kind], t_recv.at[slot, kind], across(to),
        )

    def t_on(kind):
        part = pl.ds(kind * toks, toks)
        return remote(
            T.at[1 + kind, part], T.at[3, part], t_send.at[3, kind], t_recv.at[3, kind],
            across((up_y, down_y)[kind]),
        )

    def w_own(slot, half, mat, to):
        part = pl.ds(half * half_depth, half_depth)
        return remote(
            (gw_ref, uw_ref)[mat].at[0, part], W.at[slot, part, pl.ds(mat * ff, ff)],
            w_send.at[slot, half, mat], w_recv.at[slot, half, mat], across(to),
        )

    def w_on(half, mat):
        part, cols = pl.ds(half * half_depth, half_depth), pl.ds(mat * ff, ff)
        return remote(
            W.at[1 + half, part, cols], W.at[3, part, cols],
            w_send.at[3, half, mat], w_recv.at[3, half, mat], across((up_y, down_y)[half]),
        )

    own_t = [t_own(1, 0, up_y), t_own(2, 1, down_y), t_own(1, 1, up_y), t_own(2, 0, down_y)]
    for c in own_t:
        c.start()

    tr = routes_t_ref.shape[0]
    ids = lax.broadcasted_iota(jnp.int32, (experts, toks), 0)
    chosen = jnp.zeros((experts, toks), F32)
    for k in range(tr):
        chosen = jnp.where(routes_t_ref[pl.ds(k, 1), :] == ids, 1.0, chosen)
    earlier = (
        lax.broadcasted_iota(jnp.int32, (toks, toks), 0) < lax.broadcasted_iota(jnp.int32, (toks, toks), 1)
    ).astype(F32).astype(BF16)
    place = jnp.dot(chosen.astype(BF16), earlier, preferred_element_type=F32)
    place = jnp.where(chosen > 0.5, place, -1.0)
    mine = y.astype(F32)
    place = jnp.dot(expand_ref[...], place.astype(BF16), preferred_element_type=F32) - mine
    for kind in range(2):
        hit = place == target_ref[:, pl.ds(kind, 1)]
        P1[:, pl.ds(kind * toks, toks)] = jnp.where(hit, 1.0, 0.0).astype(BF16)

    def owner(j):
        return (y, down_y, up_y, far_y)[j]

    def s1_copy(j, to, slot):
        return remote(
            S1.at[j, rows_at(to, m1)], R1.at[j, rows_at(slot, m1)],
            s1_send.at[j, to], s1_recv.at[j, slot], near(to),
        )

    def s2_copy(j, to, slot):
        cols = pl.ds(pl.multiple_of(owner(j) * qw, qw), qw)
        return remote(
            S2.at[j, rows_at(to, m2)], R2.at[rows_at(slot, m2), cols],
            s2_send.at[j, to], s2_recv.at[j, slot], along(to),
        )

    def pack(j):
        S1[j] = jnp.dot(P1[...], T[j], preferred_element_type=F32).astype(BF16)

        @pl.loop(1, nd)
        def _(k):
            s1_copy(j, lax.rem(d + k, nd), d).start()

        R1[j, rows_at(d, m1)] = S1[j, rows_at(d, m1)]

    def turn(j):
        @pl.loop(1, nd)
        def _(k):
            s = lax.rem(d + nd - k, nd)
            s1_copy(j, s, s).wait_recv()

        S2[j] = jnp.dot(perm_out_ref[...], R1[j], preferred_element_type=F32).astype(BF16)

        @pl.loop(1, nz)
        def _(k):
            s2_copy(j, lax.rem(z + k, nz), z).start()

        cols = pl.ds(pl.multiple_of(owner(j) * qw, qw), qw)
        R2[rows_at(z, m2), cols] = S2[j, rows_at(z, m2)]

    local[0].wait()
    local[1].wait()
    pack(0)
    for slot in (1, 2):
        for kind in range(2):
            t_own(slot, kind, up_y).wait_recv()
    t_on(0).start()
    t_on(1).start()
    for i in range(2):
        for mat in range(2):
            w_own(1, i, mat, up_y).start()
            w_own(2, 1 - i, mat, down_y).start()
    pack(1)
    turn(0)
    pack(2)
    turn(1)
    for kind in range(2):
        t_on(kind).wait_recv()
    pack(3)
    turn(2)

    local[2].wait()
    vec = jnp.broadcast_to(readout_ref[...], (16, depth))
    BK[0] = lax.dot_general(vec, DW[...], NT, preferred_element_type=F32)[0:8]

    def b_copy(slot, to):
        return remote(BK.at[0], BK.at[slot], b_send.at[slot], b_recv.at[slot], across(to))

    for slot, to in ((1, up_y), (2, down_y), (3, far_y)):
        b_copy(slot, to).start()

    for mat in range(2):
        for half in range(2):
            w_own(1 + half, half, mat, up_y).wait_recv()
            w_on(half, mat).start()
    turn(3)

    idl = lax.broadcasted_iota(jnp.int32, (toks, experts), 1)
    named = jnp.zeros((toks, experts), F32)
    gate = jnp.zeros((toks, experts), F32)
    for k in range(tr):
        hit = routes_ref[:, pl.ds(k, 1)] == idl
        named = jnp.where(hit, 1.0, named)
        gate = jnp.where(hit, gates_ref[:, pl.ds(k, 1)], gate)
    before = (
        lax.broadcasted_iota(jnp.int32, (toks, toks), 1) < lax.broadcasted_iota(jnp.int32, (toks, toks), 0)
    ).astype(F32).astype(BF16)
    place = jnp.dot(before, named.astype(BF16), preferred_element_type=F32)
    place = jnp.where(named > 0.5, place, -1.0)
    spread = expand_back_ref[...]
    place = jnp.dot(place.astype(BF16), spread, preferred_element_type=F32) - mine
    high = gate.astype(BF16)
    low = (gate - high.astype(F32)).astype(BF16)
    high = jnp.dot(high, spread, preferred_element_type=F32)
    low = jnp.dot(low, spread, preferred_element_type=F32)
    for half in range(2):
        hit = place == target_back_ref[pl.ds(half, 1), :]
        CB[pl.ds(2 * half * toks, toks)] = jnp.where(hit, high, 0.0).astype(BF16)
        CB[pl.ds((2 * half + 1) * toks, toks)] = jnp.where(hit, low, 0.0).astype(BF16)

    for j in range(4):
        @pl.loop(1, nz)
        def _(k):
            s = lax.rem(z + nz - k, nz)
            s2_copy(j, s, s).wait_recv()

    def block(slot):
        H[...] = jnp.dot(R2[...], W[slot], preferred_element_type=F32)
        back = BK[slot, 0:1]

        @pl.loop(0, nz // 2)
        def _(i):
            at = rows_at(i, 4 * group)
            gate_side, up_side = H[at, 0:ff], H[at, ff:]
            gate_out, up_out = [], []
            for s in range(2):
                lo = 2 * s * group
                h, dh = gate_side[lo : lo + group], gate_side[lo + group : lo + 2 * group]
                u, du = up_side[lo : lo + group], up_side[lo + group : lo + 2 * group]
                sig = jax.nn.sigmoid(h)
                first = sig * (1.0 + h * (1.0 - sig))
                second = sig * (1.0 - sig) * (2.0 + h * (1.0 - 2.0 * sig))
                gate_out.append(back * (du * first + u * second * dh))
                up_out.append(back * first * dh)
            to = rows_at(i, 2 * group)
            C[to, 0:ff] = jnp.concatenate(gate_out, 0).astype(BF16)
            C[to, ff:] = jnp.concatenate(up_out, 0).astype(BF16)

    def product(slot, n):
        part = pl.ds(pl.multiple_of(n * qw, qw), qw)
        return lax.dot_general(C[...], W[slot, part], NT, preferred_element_type=F32)

    local[3].wait()
    local[4].wait()
    block(0)
    for n in range(4):
        acc[n] = product(0, n)
    for slot in (1, 2):
        b_copy(slot, up_y).wait_recv()
        for half in range(2):
            if half != slot - 1:
                for mat in range(2):
                    w_own(slot, half, mat, up_y).wait_recv()
        block(slot)
        for n in range(4):
            acc[n] += product(slot, n)
    b_copy(3, up_y).wait_recv()
    for half in range(2):
        for mat in range(2):
            w_on(half, mat).wait_recv()
    block(3)

    for j in range(4):
        @pl.loop(1, nd)
        def _(k):
            s1_copy(j, lax.rem(d + k, nd), d).wait_send()

    def q1_copy(c, to, slot):
        return remote(
            S1.at[c, rows_at(to, m2)], Q1.at[c, rows_at(slot, m2)],
            q1_send.at[c, to], q1_recv.at[c, slot], along(to),
        )

    def q2_copy(c, to, slot):
        return remote(
            S1.at[2 + c, rows_at(to, m1)], Q2.at[c, rows_at(slot, m1)],
            q2_send.at[c, to], q2_recv.at[c, slot], near(to),
        )

    for c in range(2):
        for half in range(2):
            acc[2 * half + c] += product(3, 2 * half + c)

        @pl.loop(0, nz)
        def _(i):
            at = rows_at(i, group)
            both = jnp.concatenate([acc[c, at], acc[2 + c, at]], 0)
            S1[c, rows_at(i, m2)] = both.astype(BF16)

        @pl.loop(1, nz)
        def _(k):
            q1_copy(c, lax.rem(z + k, nz), z).start()

        Q1[c, rows_at(z, m2)] = S1[c, rows_at(z, m2)]

    for c in range(2):
        @pl.loop(1, nz)
        def _(k):
            s = lax.rem(z + nz - k, nz)
            q1_copy(c, s, s).wait_recv()

        S1[2 + c] = jnp.dot(perm_back_ref[...], Q1[c], preferred_element_type=F32).astype(BF16)

        @pl.loop(1, nd)
        def _(k):
            q2_copy(c, lax.rem(d + k, nd), d).start()

        Q2[c, rows_at(d, m1)] = S1[2 + c, rows_at(d, m1)]

    for c in range(2):
        @pl.loop(1, nd)
        def _(k):
            s = lax.rem(d + nd - k, nd)
            q2_copy(c, s, s).wait_recv()

        summed = jnp.dot(CB[...], Q2[c], preferred_element_type=F32)
        for half in range(2):
            lo = 2 * half * toks
            full = summed[lo : lo + toks] + summed[lo + toks : lo + 2 * toks]
            PTF[2 * half + c] = full
            PTB[2 * half + c] = full.astype(BF16)

    def r_copy(slot, to):
        return remote(PTB.at[to], RS.at[slot], r_send.at[slot], r_recv.at[slot], across(to))

    for slot, to in ((0, up_y), (1, down_y), (2, far_y)):
        r_copy(slot, to).start()
    total = PTF[y]
    for slot, to in ((0, up_y), (1, down_y), (2, far_y)):
        r_copy(slot, to).wait_recv()
        total = total + RS[slot].astype(F32)
    out_ref[...] = total.astype(BF16)

    for slot, to in ((0, up_y), (1, down_y), (2, far_y)):
        r_copy(slot, to).wait_send()
        b_copy(slot + 1, to).wait_send()
    for c in own_t:
        c.wait_send()
    for a in range(2):
        t_on(a).wait_send()
        for mat in range(2):
            w_own(1, a, mat, up_y).wait_send()
            w_own(2, a, mat, down_y).wait_send()
            w_on(a, mat).wait_send()
    for j in range(4):
        @pl.loop(1, nz)
        def _(k):
            s2_copy(j, lax.rem(z + k, nz), z).wait_send()
    for c in range(2):
        @pl.loop(1, nz)
        def _(k):
            q1_copy(c, lax.rem(z + k, nz), z).wait_send()

        @pl.loop(1, nd)
        def _(k):
            q2_copy(c, lax.rem(d + k, nd), d).wait_send()


def shards(near, tokens, tangents, routes, gates, gate_weight, up_weight, down_weight, readout):
    experts, parts = lax.axis_size("expert"), lax.axis_size("tensor")
    toks, qw = tokens.shape
    depth, ff = gate_weight.shape[1:]
    most = toks * routes.shape[1] * 5 // (4 * experts)
    share = most // parts
    nd, nz = near, experts // near
    rows = experts * share * 2
    expand, target, perm_out, perm_back, expand_back, target_back = tables(nz, nd, share, parts)
    hbm, vmem = pl.BlockSpec(memory_space=pl.ANY), pl.BlockSpec(memory_space=pltpu.VMEM)
    dma = pltpu.SemaphoreType.DMA
    return pl.pallas_call(
        functools.partial(kernel, (nz, nd, share, parts)),
        out_shape=jax.ShapeDtypeStruct((toks, qw), BF16),
        in_specs=[hbm] * 5 + [vmem] * 10,
        out_specs=vmem,
        scratch_shapes=[
            pltpu.VMEM((4, 2 * toks, qw), BF16),
            pltpu.VMEM((4, rows, qw), BF16),
            pltpu.VMEM((4, rows, qw), BF16),
            pltpu.VMEM((4, rows, qw), BF16),
            pltpu.VMEM((rows, depth), BF16),
            pltpu.VMEM((4, depth, 2 * ff), BF16),
            pltpu.VMEM((rows, 2 * ff), F32),
            pltpu.VMEM((rows // 2, 2 * ff), BF16),
            pltpu.VMEM((4, rows // 2, qw), F32),
            pltpu.VMEM((2, rows, qw), BF16),
            pltpu.VMEM((2, rows, qw), BF16),
            pltpu.VMEM((ff, depth), BF16),
            pltpu.VMEM((4, 8, ff), F32),
            pltpu.VMEM((4, toks, qw), F32),
            pltpu.VMEM((4, toks, qw), BF16),
            pltpu.VMEM((3, toks, qw), BF16),
            pltpu.VMEM((rows, 2 * toks), BF16),
            pltpu.VMEM((4 * toks, rows), BF16),
            dma((5,)),
            dma((4, 2)), dma((4, 2)),
            dma((4, 2, 2)), dma((4, 2, 2)),
            dma((4,)), dma((4,)),
            dma((4, nd)), dma((4, nd)),
            dma((4, nz)), dma((4, nz)),
            dma((2, nz)), dma((2, nz)),
            dma((2, nd)), dma((2, nd)),
            dma((3,)), dma((3,)),
        ],
        compiler_params=pltpu.CompilerParams(
            collective_id=0, has_side_effects=True, vmem_limit_bytes=62 * 2**20
        ),
    )(
        tokens, tangents, gate_weight, up_weight, down_weight,
        routes, routes.T, gates, readout.reshape(1, depth),
        jnp.asarray(expand, BF16), jnp.asarray(target, F32), jnp.asarray(perm_out, BF16),
        jnp.asarray(perm_back, BF16), jnp.asarray(expand_back, BF16), jnp.asarray(target_back, F32),
    )


def solution(mesh):
    return jax.shard_map(
        functools.partial(shards, NEAR),
        mesh=mesh,
        in_specs=(
            P("expert", "tensor"),
            P("expert", "tensor"),
            P("expert", None),
            P("expert", None),
            P("expert", None, "tensor"),
            P("expert", None, "tensor"),
            P("expert", "tensor", None),
            P(),
        ),
        out_specs=P("expert", "tensor"),
        check_vma=False,
    )
```

time: 455 us -> 239 us (0.53)
  waiting for transfers between devices: 294 us -> 0 us
  Pallas kernels: 0 us -> 232 us
  matrix products: 90.8 us -> 0 us
  starting transfers between devices: 20.7 us -> 0 us
  local copies, waits for them, and re-layouts: 20.2 us -> 5.78 us
  between operations: 13.4 us -> 0.01 us
  blocking collectives: 7.35 us -> 0 us
  other arithmetic: 5.22 us -> 0 us
    all_to_all x2 -> x0, waiting for transfers between devices: 235 us -> none  [the longest x1 152 us: shards(): lax.all_to_all(send, 'expert', split_axis=0, concat_axis=0, tiled=True)]
    pallas_call x0 -> x1, Pallas kernels: none -> 232 us  [shards(): pl.pallas_call(functools.partial(kernel, (nz, nd, share, parts)), out_sha...]
    dot_general x26 -> x0, matrix products: 90.8 us -> none  [the longest x4 34.1 us: shards(): lax.dot_general(coef_gate, w_gate[b], contract, preferred_element_type=jn...]
    all_gather x3 -> x0, waiting for transfers between devices: 31.7 us -> none  [the longest x1 31.7 us: shards(): lax.all_gather(jnp.stack([tokens, tangents], 0), 'tensor', axis=2, tiled=...]
    reduce_scatter x1 -> x0, waiting for transfers between devices: 26 us -> none  [shards(): lax.psum_scatter(per_token, 'tensor', scatter_dimension=1, tiled=True)]
    all_to_all x2 -> x0, starting transfers between devices: 20.6 us -> none  [the longest x1 11 us: shards(): lax.all_to_all(send, 'expert', split_axis=0, concat_axis=0, tiled=True)]
    all_to_all x2 -> x0, local copies, waits for them, and re-layouts: 12.7 us -> none  [the longest x1 8.2 us: shards(): lax.all_to_all(send, 'expert', split_axis=0, concat_axis=0, tiled=True)]
    all_gather x1 -> x0, blocking collectives: 7.35 us -> none  [shards(): back = lax.all_gather(back, 'tensor', axis=0)]
  transfers between devices with their start and end apart: 6 -> 0, of which waited for: 4 -> 0; matrix products, arithmetic and copies ran while one was open for 5% -> 0% of each run, Pallas kernels for 0% -> 0%
where the time goes in v2:
time: 239 us; the launch traced here: 237 us
  Pallas kernels  232 us (97%)
  local copies, waits for them, and re-layouts  5.78 us (2%)
    pallas_call x1, Pallas kernels, shards(): pl.pallas_call(functools.partial(kernel, (nz, nd, share, parts)), out_sha...  232 us

profile of v2, /device:TPU:9, one launch (start us, length us, event | category | flops | bytes accessed | tf_op | source)
XLA Modules:
  0.0 237.4 jit_solution(17717446782910113268)
XLA Ops:
  0.0 1.3 reshape.3.readout_ref
  1.3 1.4 copy.16.gates_ref
  2.7 1.4 copy.15.routes_ref
  4.1 231.7 %shard_map.136 = bf16[128,896]{1,0:T(8,128)(2,1)} custom-call(bf16[128,896]{1,0:T(8,128)(2,1)} %tok_ref.1, bf16[128,896]{1,0:T(8,128)(2,1)} %tan_ref.1, bf16[1,3584,256]{2,1,0:T(8,128)(2,1)} %gw_ref.1, bf16[1,3584,256]{2,1,0:T(8,128)(2,1)} %uw_ref.1, bf16[1,256,3584]{2,1,0:T(8,128)(2,1)} %dw_ref.1, s32[128,8]{1,0:T(8,128)} %copy.15.routes_ref, ...), custom_call_target="tpu_custom_call" | custom-call | tf_op jit(solution)/shard_map/pallas_call | solution.py:411
  235.8 1.6 copy.18

commit v3 on v2

v3 whole, which is shorter than its diff:
```python
import functools

import jax
import jax.numpy as jnp
import numpy as np
from jax import lax
from jax.experimental import pallas as pl
from jax.experimental.pallas import tpu as pltpu
from jax.sharding import PartitionSpec as P

MESH = pl.DeviceIdType.MESH
NEAR = 8
F32 = jnp.float32
BF16 = jnp.bfloat16
NT = (((1,), (1,)), ((), ()))


def tables(nz, nd, share, parts):
    rows = nz * nd * 2 * share
    experts = nz * nd
    expand = np.zeros((2, rows, experts), np.float32)
    target = np.full((rows, 2), -100.0, np.float32)
    to_z = np.zeros((rows, rows), np.float32)
    expand_back = np.zeros((2, experts, rows), np.float32)
    target_back = np.full((8, rows), -100.0, np.float32)
    for z in range(nz):
        for d in range(nd):
            for k in range(2):
                for q in range(share):
                    by_z = ((z * 2 + k) * nd + d) * share + q
                    by_d = ((d * 2 + k) * nz + z) * share + q
                    for own in range(2):
                        e = z * nd + d // 2 * 2 + own
                        expand[own, by_z, e] = 1
                        expand_back[own, e, by_d] = 1
                    target[by_z, k] = parts * q + d % 2
                    target_back[k, by_d] = parts * q + d % 2
                    to_z[by_z, by_d] = 1
    return expand, target, to_z, to_z.T, expand_back, target_back


def kernel(
    dims,
    tok_ref, tan_ref, gw_ref, uw_ref, dw_ref,
    routes_ref, routes_t_ref, gates_ref, readout_ref,
    expand_ref, target_ref, to_z_ref, to_d_ref, expand_back_ref, target_back_ref,
    out_ref,
    T, S1, R1, S2, R2, W, H, C, A, Q1, Q2, DW, BO, BK, PTF, PTB, RS, X0, PZ, PD, CB,
    local_sem, t_send, t_recv, w_send, w_recv, b_send, b_recv,
    s1_send, s1_recv, s2_send, s2_recv, q1_send, q1_recv, q2_send, q2_recv, r_send, r_recv,
):
    nz, nd, share, parts = dims
    toks, qw = tok_ref.shape
    depth, ff = gw_ref.shape[1:]
    half_depth = depth // 2
    experts = nz * nd
    m1, m2 = nz * 2 * share, nd * 2 * share
    group = nd * share
    me, y = lax.axis_index("expert"), lax.axis_index("tensor")
    z, d = me // nd, lax.rem(me, nd)
    own, odd, core = y // 2, lax.rem(y, 2), lax.rem(me, 2)
    home = core == own
    away = core != own
    mate, outer, far = y + 1 - 2 * odd, parts - 1 - y, lax.rem(y + 2, parts)
    others = (mate, outer, far)

    def near(dd):
        return (z * nd + dd, y)

    def along(zz):
        return (zz * nd + d, y)

    def across(yy, cc=None):
        return (me if cc is None else me - core + cc, yy)

    def rows_at(i, n):
        return pl.ds(pl.multiple_of(i * n, n), n)

    def remote(src, dst, ss, rs, dev):
        return pltpu.make_async_remote_copy(
            src_ref=src, dst_ref=dst, send_sem=ss, recv_sem=rs, device_id=dev, device_id_type=MESH
        )

    barrier = pltpu.get_barrier_semaphore()
    for yy in others:
        for cc in range(2):
            pl.semaphore_signal(barrier, inc=1, device_id=across(yy, cc), device_id_type=MESH)

    @pl.loop(1, nd)
    def _(k):
        pl.semaphore_signal(barrier, inc=1, device_id=near(lax.rem(d + k, nd)), device_id_type=MESH)

    @pl.loop(1, nz)
    def _(k):
        pl.semaphore_signal(barrier, inc=1, device_id=along(lax.rem(z + k, nz)), device_id_type=MESH)

    local = [
        pltpu.make_async_copy(tok_ref, T.at[0, pl.ds(0, toks)], local_sem.at[0]),
        pltpu.make_async_copy(tan_ref, T.at[0, pl.ds(toks, toks)], local_sem.at[1]),
        pltpu.make_async_copy(dw_ref.at[0], DW, local_sem.at[2]),
    ]
    stage = [
        pltpu.make_async_copy(gw_ref.at[0], W.at[0, :, pl.ds(0, ff)], local_sem.at[3]),
        pltpu.make_async_copy(uw_ref.at[0], W.at[0, :, pl.ds(ff, ff)], local_sem.at[4]),
    ]
    for c in local:
        c.start()

    @pl.when(home)
    def _():
        for c in stage:
            c.start()

    pl.semaphore_wait(barrier, 2 * 3 + nd - 1 + nz - 1)

    def t_own(slot, kind):
        return remote(
            (tok_ref, tan_ref)[kind], T.at[slot, pl.ds(kind * toks, toks)],
            t_send.at[slot, kind], t_recv.at[slot, kind], across(others[slot - 1]),
        )

    def t_on():
        return remote(T.at[1], T.at[3], t_send.at[3, 0], t_recv.at[3, 0], across(outer))

    def w_from(slot, half, mat, yy, cc, sem):
        part = pl.ds(half * half_depth, half_depth)
        return remote(
            (gw_ref, uw_ref)[mat].at[0, part], W.at[slot, part, pl.ds(mat * ff, ff)],
            w_send.at[sem, half, mat], w_recv.at[slot, half, mat], across(yy, cc),
        )

    def w_on(slot, half, mat, slot_to, yy, cc, sem):
        part, cols = pl.ds(pl.multiple_of(half * half_depth, half_depth), half_depth), pl.ds(mat * ff, ff)
        return remote(
            W.at[slot, part, cols], W.at[slot_to, part, cols],
            w_send.at[sem, half, mat], w_recv.at[slot_to, half, mat], across(yy, cc),
        )

    pieces = [(half, mat) for mat in range(2) for half in range(2)]
    for slot in (1, 2):
        for kind in range(2):
            t_own(slot, kind).start()

    @pl.when(home)
    def _():
        for half, mat in pieces:
            w_from(1, half, mat, mate, half, 0).start()
        for half, mat in pieces:
            w_from(0, half, mat, y, 1 - core, 1).start()

    @pl.when(away)
    def _():
        for half, mat in pieces:
            w_from(2, half, mat, outer, half, 0).start()

    def w_get(slot, half, mat):
        w_on(slot, half, mat, slot, y, 1 - core, slot + 1).wait_recv()

    def pass_on(slot, mat):
        w_get(slot, core, mat)
        w_on(slot, core, mat, slot, y, 1 - core, slot + 1).start()
        if slot == 2:
            w_on(2, core, mat, 3, mate, core, 5).start()

    tr = routes_t_ref.shape[0]
    ids = lax.broadcasted_iota(jnp.int32, (experts, toks), 0)
    chosen = jnp.zeros((experts, toks), F32)
    for k in range(tr):
        chosen = jnp.where(routes_t_ref[pl.ds(k, 1), :] == ids, 1.0, chosen)
    earlier = (
        lax.broadcasted_iota(jnp.int32, (toks, toks), 0) < lax.broadcasted_iota(jnp.int32, (toks, toks), 1)
    ).astype(F32).astype(BF16)
    place = jnp.dot(chosen.astype(BF16), earlier, preferred_element_type=F32)
    place = jnp.where(chosen > 0.5, place, -1.0)
    mine = (2 * odd).astype(F32)
    place = jnp.dot(expand_ref[own], place.astype(BF16), preferred_element_type=F32) - mine
    for kind in range(2):
        hit = place == target_ref[:, pl.ds(kind, 1)]
        PZ[:, pl.ds(kind * toks, toks)] = jnp.where(hit, 1.0, 0.0).astype(BF16)

    def owner(j):
        return (y, mate, outer, far)[j]

    def cols_of(j):
        return pl.ds(pl.multiple_of(owner(j) * qw, qw), qw)

    def s1_copy(j, to, slot):
        at = rows_at(slot, m1)
        return remote(
            S1.at[j, rows_at(to, m1)], R1.at[j, at] if j else X0.at[at],
            s1_send.at[j, to], s1_recv.at[j, slot], near(to),
        )

    def s2_copy(j, to, slot):
        at = rows_at(slot, m2)
        return remote(
            S2.at[j, rows_at(to, m2)], R2.at[at, cols_of(j)] if j else R1.at[0, at],
            s2_send.at[j, to], s2_recv.at[j, slot], along(to),
        )

    def send_near(copy, j):
        @pl.loop(1, nd)
        def _(k):
            copy(j, lax.rem(d + k, nd), d).start()

    def send_along(copy, j):
        @pl.loop(1, nz)
        def _(k):
            copy(j, lax.rem(z + k, nz), z).start()

    def get_near(copy, j):
        @pl.loop(1, nd)
        def _(k):
            s = lax.rem(d + nd - k, nd)
            copy(j, s, s).wait_recv()

    def get_along(copy, j):
        @pl.loop(1, nz)
        def _(k):
            s = lax.rem(z + nz - k, nz)
            copy(j, s, s).wait_recv()

    def sent_near(copy, j):
        @pl.loop(1, nd)
        def _(k):
            copy(j, lax.rem(d + k, nd), d).wait_send()

    def sent_along(copy, j):
        @pl.loop(1, nz)
        def _(k):
            copy(j, lax.rem(z + k, nz), z).wait_send()

    def mix(table, rows):
        return jnp.dot(table, rows, preferred_element_type=F32).astype(BF16)

    def pack(j):
        S1[j] = mix(PD[...], T[j])
        send_near(s1_copy, j)
        R1[j, rows_at(d, m1)] = S1[j, rows_at(d, m1)]

    def turn(j):
        get_near(s1_copy, j)
        S2[j] = mix(to_z_ref[...], R1[j])
        send_along(s2_copy, j)
        R2[rows_at(z, m2), cols_of(j)] = S2[j, rows_at(z, m2)]

    local[0].wait()
    local[1].wait()
    S2[0] = mix(PZ[...], T[0])
    send_along(s2_copy, 0)
    R1[0, rows_at(z, m2)] = S2[0, rows_at(z, m2)]
    PD[...] = mix(to_d_ref[...], PZ[...])

    local[2].wait()
    vec = jnp.broadcast_to(readout_ref[...], (16, depth))
    BO[...] = lax.dot_general(vec, DW[...], NT, preferred_element_type=F32)[0:8]

    def b_copy(slot, i, yy, cc):
        return remote(BO, BK.at[slot], b_send.at[i], b_recv.at[slot], across(yy, cc))

    def b_home():
        return [b_copy(0, 0, y, 1 - core), b_copy(1, 1, mate, 0), b_copy(1, 2, mate, 1)]

    def b_away():
        return [b_copy(slot, 2 * slot - 4 + cc, yy, cc) for slot, yy in ((2, outer), (3, far)) for cc in range(2)]

    @pl.when(home)
    def _():
        for c in b_home():
            c.start()
        BK[0] = BO[...]

    @pl.when(away)
    def _():
        for c in b_away():
            c.start()

    for kind in range(2):
        t_own(1, kind).wait_recv()
    t_on().start()
    pack(1)
    for kind in range(2):
        t_own(2, kind).wait_recv()
    turn(1)
    pack(2)
    pass_on(2, 0)
    t_on().wait_recv()
    pack(3)
    turn(2)
    pass_on(2, 1)
    pass_on(1, 0)
    get_along(s2_copy, 0)
    S1[0] = mix(to_d_ref[...], R1[0])
    send_near(s1_copy, 0)
    X0[rows_at(d, m1)] = S1[0, rows_at(d, m1)]
    turn(3)
    pass_on(1, 1)

    idl = lax.broadcasted_iota(jnp.int32, (toks, experts), 1)
    named = jnp.zeros((toks, experts), F32)
    gate = jnp.zeros((toks, experts), F32)
    for k in range(tr):
        hit = routes_ref[:, pl.ds(k, 1)] == idl
        named = jnp.where(hit, 1.0, named)
        gate = jnp.where(hit, gates_ref[:, pl.ds(k, 1)], gate)
    before = (
        lax.broadcasted_iota(jnp.int32, (toks, toks), 1) < lax.broadcasted_iota(jnp.int32, (toks, toks), 0)
    ).astype(F32).astype(BF16)
    place = jnp.dot(before, named.astype(BF16), preferred_element_type=F32)
    place = jnp.where(named > 0.5, place, -1.0)
    spread = expand_back_ref[own]
    place = jnp.dot(place.astype(BF16), spread, preferred_element_type=F32) - mine
    high = gate.astype(BF16)
    low = (gate - high.astype(F32)).astype(BF16)
    high = jnp.dot(high, spread, preferred_element_type=F32)
    low = jnp.dot(low, spread, preferred_element_type=F32)
    for half in range(2):
        hit = place == target_back_ref[pl.ds(half, 1), :]
        CB[0, pl.ds(2 * half * toks, toks)] = jnp.where(hit, high, 0.0).astype(BF16)
        CB[0, pl.ds((2 * half + 1) * toks, toks)] = jnp.where(hit, low, 0.0).astype(BF16)
    CB[1] = mix(CB[0], to_d_ref[...])

    get_near(s1_copy, 0)
    R2[:, cols_of(0)] = mix(to_z_ref[...], X0[...])

    pass_on(3, 0)
    pass_on(3, 1)

    @pl.when(home)
    def _():
        for c in stage:
            c.wait()

    @pl.when(away)
    def _():
        for half, mat in pieces:
            w_get(0, half, mat)
        b_copy(0, 0, y, 1 - core).wait_recv()

    for slot in (1, 2, 3):
        for mat in range(2):
            w_get(slot, 1 - core, mat)
        b_copy(slot, 0, y, 1 - core).wait_recv()

    for j in range(4):
        if j:
            get_along(s2_copy, j)
        cols = cols_of(j)
        for slot in range(4):
            H[slot] = (H[slot] if j else 0.0) + jnp.dot(R2[:, cols], W[slot, cols], preferred_element_type=F32)

    for slot in range(4):
        back = BK[slot, 0:1]

        @pl.loop(0, nz // 2)
        def _(i):
            at = rows_at(i, 4 * group)
            gate_side, up_side = H[slot, at, 0:ff], H[slot, at, ff:]
            gate_out, up_out = [], []
            for s in range(2):
                lo = 2 * s * group
                h, dh = gate_side[lo : lo + group], gate_side[lo + group : lo + 2 * group]
                u, du = up_side[lo : lo + group], up_side[lo + group : lo + 2 * group]
                sig = jax.nn.sigmoid(h)
                first = sig * (1.0 + h * (1.0 - sig))
                second = sig * (1.0 - sig) * (2.0 + h * (1.0 - 2.0 * sig))
                gate_out.append(back * (du * first + u * second * dh))
                up_out.append(back * first * dh)
            to = rows_at(i, 2 * group)
            C[slot, to, 0:ff] = jnp.concatenate(gate_out, 0).astype(BF16)
            C[slot, to, ff:] = jnp.concatenate(up_out, 0).astype(BF16)

    def product(n):
        total = 0.0
        for slot in range(4):
            total = total + lax.dot_general(
                C[slot], W[slot, pl.ds(n * qw, qw)], NT, preferred_element_type=F32
            )
        return total

    for j in range(4):
        sent_near(s1_copy, j)

    def q1_copy(c, to, slot):
        return remote(
            S1.at[c, rows_at(to, m2)], Q1.at[c, rows_at(slot, m2)],
            q1_send.at[c, to], q1_recv.at[c, slot], along(to),
        )

    def q2_copy(c, to, slot):
        return remote(
            S1.at[2 + c, rows_at(to, m1)], Q2.at[c, rows_at(slot, m1)],
            q2_send.at[c, to], q2_recv.at[c, slot], near(to),
        )

    def go_along(c):
        send_along(q1_copy, c)
        Q1[c, rows_at(z, m2)] = S1[c, rows_at(z, m2)]

    def go_near(c, rows):
        S1[2 + c] = mix(to_d_ref[...], rows)
        send_near(q2_copy, c)
        Q2[c, rows_at(d, m1)] = S1[2 + c, rows_at(d, m1)]

    def r_copy(slot, to):
        return remote(PTB.at[to], RS.at[slot], r_send.at[slot], r_recv.at[slot], across(to))

    def combine(c, rows):
        summed = jnp.dot(CB[c], rows, preferred_element_type=F32)
        for half in range(2):
            lo = 2 * half * toks
            full = summed[lo : lo + toks] + summed[lo + toks : lo + 2 * toks]
            PTF[2 * half + c] = full
            PTB[2 * half + c] = full.astype(BF16)
        for slot, to in enumerate(others):
            @pl.when(lax.rem(to, 2) == c)
            def _():
                r_copy(slot, to).start()

    for c in range(2):
        for half in range(2):
            A[half] = product(2 * half + c)

        @pl.loop(0, nz)
        def _(i):
            at = rows_at(i, group)
            both = jnp.concatenate([A[0, at], A[1, at]], 0)
            S1[c, rows_at(i, m2)] = both.astype(BF16)

        if c == 0:
            go_along(0)
        else:
            go_near(1, S1[1])
    get_near(q2_copy, 1)
    S1[1] = mix(to_z_ref[...], Q2[1])
    go_along(1)
    get_along(q1_copy, 0)
    go_near(0, Q1[0])
    get_near(q2_copy, 0)
    combine(0, Q2[0])
    get_along(q1_copy, 1)
    combine(1, Q1[1])

    total = PTF[y]
    for slot, to in enumerate(others):
        r_copy(slot, to).wait_recv()
        total = total + RS[slot].astype(F32)
    out_ref[...] = total.astype(BF16)

    for slot, to in enumerate(others):
        r_copy(slot, to).wait_send()
    for slot in (1, 2):
        for kind in range(2):
            t_own(slot, kind).wait_send()
    t_on().wait_send()

    @pl.when(home)
    def _():
        for half, mat in pieces:
            w_from(1, half, mat, mate, half, 0).wait_send()
            w_from(0, half, mat, y, 1 - core, 1).wait_send()
        for c in b_home():
            c.wait_send()

    @pl.when(away)
    def _():
        for half, mat in pieces:
            w_from(2, half, mat, outer, half, 0).wait_send()
        for c in b_away():
            c.wait_send()

    for mat in range(2):
        for slot in (1, 2, 3):
            w_on(slot, core, mat, slot, y, 1 - core, slot + 1).wait_send()
        w_on(2, core, mat, 3, mate, core, 5).wait_send()
    for j in range(4):
        sent_along(s2_copy, j)
    for c in range(2):
        sent_along(q1_copy, c)
        sent_near(q2_copy, c)


def shards(near, tokens, tangents, routes, gates, gate_weight, up_weight, down_weight, readout):
    experts, parts = lax.axis_size("expert"), lax.axis_size("tensor")
    toks, qw = tokens.shape
    depth, ff = gate_weight.shape[1:]
    most = toks * routes.shape[1] * 5 // (4 * experts)
    share = most // parts
    nd, nz = near, experts // near
    rows = experts * share * 2
    expand, target, to_z, to_d, expand_back, target_back = tables(nz, nd, share, parts)
    hbm, vmem = pl.BlockSpec(memory_space=pl.ANY), pl.BlockSpec(memory_space=pltpu.VMEM)
    dma = pltpu.SemaphoreType.DMA
    return pl.pallas_call(
        functools.partial(kernel, (nz, nd, share, parts)),
        out_shape=jax.ShapeDtypeStruct((toks, qw), BF16),
        in_specs=[hbm] * 5 + [vmem] * 10,
        out_specs=vmem,
        scratch_shapes=[
            pltpu.VMEM((4, 2 * toks, qw), BF16),
            pltpu.VMEM((4, rows, qw), BF16),
            pltpu.VMEM((4, rows, qw), BF16),
            pltpu.VMEM((4, rows, qw), BF16),
            pltpu.VMEM((rows, depth), BF16),
            pltpu.VMEM((4, depth, 2 * ff), BF16),
            pltpu.VMEM((4, rows, 2 * ff), F32),
            pltpu.VMEM((4, rows // 2, 2 * ff), BF16),
            pltpu.VMEM((2, rows // 2, qw), F32),
            pltpu.VMEM((2, rows, qw), BF16),
            pltpu.VMEM((2, rows, qw), BF16),
            pltpu.VMEM((ff, depth), BF16),
            pltpu.VMEM((8, ff), F32),
            pltpu.VMEM((4, 8, ff), F32),
            pltpu.VMEM((4, toks, qw), F32),
            pltpu.VMEM((4, toks, qw), BF16),
            pltpu.VMEM((3, toks, qw), BF16),
            pltpu.VMEM((rows, qw), BF16),
            pltpu.VMEM((rows, 2 * toks), BF16),
            pltpu.VMEM((rows, 2 * toks), BF16),
            pltpu.VMEM((2, 4 * toks, rows), BF16),
            dma((5,)),
            dma((4, 2)), dma((4, 2)),
            dma((6, 2, 2)), dma((4, 2, 2)),
            dma((4,)), dma((4,)),
            dma((4, nd)), dma((4, nd)),
            dma((4, nz)), dma((4, nz)),
            dma((2, nz)), dma((2, nz)),
            dma((2, nd)), dma((2, nd)),
            dma((3,)), dma((3,)),
        ],
        compiler_params=pltpu.CompilerParams(
            collective_id=0, has_side_effects=True, vmem_limit_bytes=62 * 2**20
        ),
    )(
        tokens, tangents, gate_weight, up_weight, down_weight,
        routes, routes.T, gates, readout.reshape(1, depth),
        jnp.asarray(expand, BF16), jnp.asarray(target, F32), jnp.asarray(to_z, BF16),
        jnp.asarray(to_d, BF16), jnp.asarray(expand_back, BF16), jnp.asarray(target_back, F32),
    )


def solution(mesh):
    return jax.shard_map(
        functools.partial(shards, NEAR),
        mesh=mesh,
        in_specs=(
            P("expert", "tensor"),
            P("expert", "tensor"),
            P("expert", None),
            P("expert", None),
            P("expert", None, "tensor"),
            P("expert", None, "tensor"),
            P("expert", "tensor", None),
            P(),
        ),
        out_specs=P("expert", "tensor"),
        check_vma=False,
    )
```

time: 239 us -> 194 us (0.81)
  Pallas kernels: 232 us -> 188 us
    pallas_call x1, Pallas kernels: 232 us -> 188 us  [shards(): pl.pallas_call(functools.partial(kernel, (nz, nd, share, parts)), out_sha...]
where the time goes in v3:
time: 194 us; the launch traced here: 193 us
  Pallas kernels  188 us (97%)
  local copies, waits for them, and re-layouts  5.78 us (3%)
    pallas_call x1, Pallas kernels, shards(): pl.pallas_call(functools.partial(kernel, (nz, nd, share, parts)), out_sha...  188 us
    unnamed x3, local copies, waits for them, and re-layouts  4.47 us

profile of v3, /device:TPU:9, one launch (start us, length us, event | category | flops | bytes accessed | tf_op | source)
XLA Modules:
  0.0 193.4 jit_solution(12257326773286279301)
XLA Ops:
  0.0 1.3 reshape.3.readout_ref
  1.3 1.4 copy.16.gates_ref
  2.7 1.4 copy.15.routes_ref
  4.1 187.6 %shard_map.136 = bf16[128,896]{1,0:T(8,128)(2,1)} custom-call(bf16[128,896]{1,0:T(8,128)(2,1)} %tok_ref.1, bf16[128,896]{1,0:T(8,128)(2,1)} %tan_ref.1, bf16[1,3584,256]{2,1,0:T(8,128)(2,1)} %gw_ref.1, bf16[1,3584,256]{2,1,0:T(8,128)(2,1)} %uw_ref.1, bf16[1,256,3584]{2,1,0:T(8,128)(2,1)} %dw_ref.1, s32[128,8]{1,0:T(8,128)} %copy.15.routes_ref, ...), custom_call_target="tpu_custom_call" | custom-call | tf_op jit(solution)/shard_map/pallas_call | solution.py:494
  191.7 1.6 copy.18

commit v4 on v3

--- a/solution.py
+++ b/solution.py
@@ -42,10 +42,10 @@
 def kernel(
     dims,
     tok_ref, tan_ref, gw_ref, uw_ref, dw_ref,
-    routes_ref, routes_t_ref, gates_ref, readout_ref,
-    expand_ref, target_ref, to_z_ref, to_d_ref, expand_back_ref, target_back_ref,
+    routes_ref, gates_ref, readout_ref,
+    expand_ref, target_ref, to_z_hbm, to_d_hbm, expand_back_ref, target_back_ref,
     out_ref,
-    T, S1, R1, S2, R2, W, H, C, A, Q1, Q2, DW, BO, BK, PTF, PTB, RS, X0, PZ, PD, CB,
+    T, S1, R1, S2, R2, W, H, C, A, Q1, Q2, DW, BO, BK, PTF, PTB, RS, X0, PZ, PD, CB, to_z_ref, to_d_ref,
     local_sem, t_send, t_recv, w_send, w_recv, b_send, b_recv,
     s1_send, s1_recv, s2_send, s2_recv, q1_send, q1_recv, q2_send, q2_recv, r_send, r_recv,
 ):
@@ -98,6 +98,8 @@
         pltpu.make_async_copy(tok_ref, T.at[0, pl.ds(0, toks)], local_sem.at[0]),
         pltpu.make_async_copy(tan_ref, T.at[0, pl.ds(toks, toks)], local_sem.at[1]),
         pltpu.make_async_copy(dw_ref.at[0], DW, local_sem.at[2]),
+        pltpu.make_async_copy(to_d_hbm, to_d_ref, local_sem.at[5]),
+        pltpu.make_async_copy(to_z_hbm, to_z_ref, local_sem.at[6]),
     ]
     stage = [
         pltpu.make_async_copy(gw_ref.at[0], W.at[0, :, pl.ds(0, ff)], local_sem.at[3]),
@@ -111,8 +113,6 @@
         for c in stage:
             c.start()
 
-    pl.semaphore_wait(barrier, 2 * 3 + nd - 1 + nz - 1)
-
     def t_own(slot, kind):
         return remote(
             (tok_ref, tan_ref)[kind], T.at[slot, pl.ds(kind * toks, toks)],
@@ -137,21 +137,6 @@
         )
 
     pieces = [(half, mat) for mat in range(2) for half in range(2)]
-    for slot in (1, 2):
-        for kind in range(2):
-            t_own(slot, kind).start()
-
-    @pl.when(home)
-    def _():
-        for half, mat in pieces:
-            w_from(1, half, mat, mate, half, 0).start()
-        for half, mat in pieces:
-            w_from(0, half, mat, y, 1 - core, 1).start()
-
-    @pl.when(away)
-    def _():
-        for half, mat in pieces:
-            w_from(2, half, mat, outer, half, 0).start()
 
     def w_get(slot, half, mat):
         w_on(slot, half, mat, slot, y, 1 - core, slot + 1).wait_recv()
@@ -162,18 +147,18 @@
         if slot == 2:
             w_on(2, core, mat, 3, mate, core, 5).start()
 
-    tr = routes_t_ref.shape[0]
+    top = routes_ref.shape[0]
     ids = lax.broadcasted_iota(jnp.int32, (experts, toks), 0)
     chosen = jnp.zeros((experts, toks), F32)
-    for k in range(tr):
-        chosen = jnp.where(routes_t_ref[pl.ds(k, 1), :] == ids, 1.0, chosen)
+    for k in range(top):
+        chosen = jnp.where(routes_ref[pl.ds(k, 1), :] == ids, 1.0, chosen)
     earlier = (
         lax.broadcasted_iota(jnp.int32, (toks, toks), 0) < lax.broadcasted_iota(jnp.int32, (toks, toks), 1)
     ).astype(F32).astype(BF16)
     place = jnp.dot(chosen.astype(BF16), earlier, preferred_element_type=F32)
-    place = jnp.where(chosen > 0.5, place, -1.0)
+    taken = jnp.where(chosen > 0.5, place, -1.0).astype(BF16)
     mine = (2 * odd).astype(F32)
-    place = jnp.dot(expand_ref[own], place.astype(BF16), preferred_element_type=F32) - mine
+    place = jnp.dot(expand_ref[own], taken, preferred_element_type=F32) - mine
     for kind in range(2):
         hit = place == target_ref[:, pl.ds(kind, 1)]
         PZ[:, pl.ds(kind * toks, toks)] = jnp.where(hit, 1.0, 0.0).astype(BF16)
@@ -247,12 +232,31 @@
     local[0].wait()
     local[1].wait()
     S2[0] = mix(PZ[...], T[0])
+    pl.semaphore_wait(barrier, 2 * 3 + nd - 1 + nz - 1)
     send_along(s2_copy, 0)
+    for slot in (1, 2):
+        for kind in range(2):
+            t_own(slot, kind).start()
+
+    @pl.when(home)
+    def _():
+        for half, mat in pieces:
+            w_from(1, half, mat, mate, half, 0).start()
+        for half, mat in pieces:
+            w_from(0, half, mat, y, 1 - core, 1).start()
+
+    @pl.when(away)
+    def _():
+        for half, mat in pieces:
+            w_from(2, half, mat, outer, half, 0).start()
+
     R1[0, rows_at(z, m2)] = S2[0, rows_at(z, m2)]
+    local[3].wait()
+    local[4].wait()
     PD[...] = mix(to_d_ref[...], PZ[...])
 
     local[2].wait()
-    vec = jnp.broadcast_to(readout_ref[...], (16, depth))
+    vec = jnp.broadcast_to(readout_ref[...][None, :], (16, depth))
     BO[...] = lax.dot_general(vec, DW[...], NT, preferred_element_type=F32)[0:8]
 
     def b_copy(slot, i, yy, cc):
@@ -296,24 +300,16 @@
     turn(3)
     pass_on(1, 1)
 
-    idl = lax.broadcasted_iota(jnp.int32, (toks, experts), 1)
-    named = jnp.zeros((toks, experts), F32)
-    gate = jnp.zeros((toks, experts), F32)
-    for k in range(tr):
-        hit = routes_ref[:, pl.ds(k, 1)] == idl
-        named = jnp.where(hit, 1.0, named)
-        gate = jnp.where(hit, gates_ref[:, pl.ds(k, 1)], gate)
-    before = (
-        lax.broadcasted_iota(jnp.int32, (toks, toks), 1) < lax.broadcasted_iota(jnp.int32, (toks, toks), 0)
-    ).astype(F32).astype(BF16)
-    place = jnp.dot(before, named.astype(BF16), preferred_element_type=F32)
-    place = jnp.where(named > 0.5, place, -1.0)
-    spread = expand_back_ref[own]
-    place = jnp.dot(place.astype(BF16), spread, preferred_element_type=F32) - mine
+    gate = jnp.zeros((experts, toks), F32)
+    for k in range(top):
+        gate = jnp.where(routes_ref[pl.ds(k, 1), :] == ids, gates_ref[pl.ds(k, 1), :], gate)
     high = gate.astype(BF16)
     low = (gate - high.astype(F32)).astype(BF16)
-    high = jnp.dot(high, spread, preferred_element_type=F32)
-    low = jnp.dot(low, spread, preferred_element_type=F32)
+    place, high, low = [
+        lax.dot_general(a, expand_back_ref[own], (((0,), (0,)), ((), ())), preferred_element_type=F32)
+        for a in (taken, high, low)
+    ]
+    place = place - mine
     for half in range(2):
         hit = place == target_back_ref[pl.ds(half, 1), :]
         CB[0, pl.ds(2 * half * toks, toks)] = jnp.where(hit, high, 0.0).astype(BF16)
@@ -352,9 +348,8 @@
     for slot in range(4):
         back = BK[slot, 0:1]
 
-        @pl.loop(0, nz // 2)
-        def _(i):
-            at = rows_at(i, 4 * group)
+        for i in range(nz // 2):
+            at = pl.ds(i * 4 * group, 4 * group)
             gate_side, up_side = H[slot, at, 0:ff], H[slot, at, ff:]
             gate_out, up_out = [], []
             for s in range(2):
@@ -366,26 +361,39 @@
                 second = sig * (1.0 - sig) * (2.0 + h * (1.0 - 2.0 * sig))
                 gate_out.append(back * (du * first + u * second * dh))
                 up_out.append(back * first * dh)
-            to = rows_at(i, 2 * group)
+            to = pl.ds(i * 2 * group, 2 * group)
             C[slot, to, 0:ff] = jnp.concatenate(gate_out, 0).astype(BF16)
             C[slot, to, ff:] = jnp.concatenate(up_out, 0).astype(BF16)
 
-    def product(n):
+    def product(n, cols):
+        lo, hi = cols
         total = 0.0
         for slot in range(4):
             total = total + lax.dot_general(
-                C[slot], W[slot, pl.ds(n * qw, qw)], NT, preferred_element_type=F32
+                C[slot], W[slot, pl.ds(n * qw + lo, hi - lo)], NT, preferred_element_type=F32
             )
         return total
 
     for j in range(4):
         sent_near(s1_copy, j)
 
-    def q1_copy(c, to, slot):
-        return remote(
-            S1.at[c, rows_at(to, m2)], Q1.at[c, rows_at(slot, m2)],
-            q1_send.at[c, to], q1_recv.at[c, slot], along(to),
-        )
+    short = (qw // 128 * 2 // 7 or 1) * 128
+    spans = [[(0, short), (short, qw)], [(0, qw - short), (qw - short, qw)]]
+    if short == qw:
+        spans = [[(0, qw // 2), (qw // 2, qw)]] * 2
+
+    def span(c, i):
+        lo, hi = spans[c][i]
+        return pl.ds(lo, hi - lo)
+
+    def q1_piece(c, i):
+        def q1_copy(_, to, slot):
+            return remote(
+                S1.at[c, rows_at(to, m2), span(c, i)], Q1.at[c, rows_at(slot, m2), span(c, i)],
+                q1_send.at[c, i, to], q1_recv.at[c, i, slot], along(to),
+            )
+
+        return q1_copy
 
     def q2_copy(c, to, slot):
         return remote(
@@ -393,62 +401,82 @@
             q2_send.at[c, to], q2_recv.at[c, slot], near(to),
         )
 
-    def go_along(c):
-        send_along(q1_copy, c)
-        Q1[c, rows_at(z, m2)] = S1[c, rows_at(z, m2)]
+    def go_along(c, i):
+        send_along(q1_piece(c, i), c)
+        Q1[c, rows_at(z, m2), span(c, i)] = S1[c, rows_at(z, m2), span(c, i)]
 
     def go_near(c, rows):
         S1[2 + c] = mix(to_d_ref[...], rows)
         send_near(q2_copy, c)
         Q2[c, rows_at(d, m1)] = S1[2 + c, rows_at(d, m1)]
 
-    def r_copy(slot, to):
-        return remote(PTB.at[to], RS.at[slot], r_send.at[slot], r_recv.at[slot], across(to))
-
-    def combine(c, rows):
+    def r_piece(c, i, slot, to):
+        def r_copy():
+            return remote(
+                PTB.at[to, :, span(c, i)], RS.at[slot, :, span(c, i)],
+                r_send.at[slot, i], r_recv.at[slot, i], across(to),
+            )
+
+        return r_copy()
+
+    def combine(c, i, rows):
         summed = jnp.dot(CB[c], rows, preferred_element_type=F32)
         for half in range(2):
             lo = 2 * half * toks
             full = summed[lo : lo + toks] + summed[lo + toks : lo + 2 * toks]
-            PTF[2 * half + c] = full
-            PTB[2 * half + c] = full.astype(BF16)
+            PTF[2 * half + c, :, span(c, i)] = full
+            PTB[2 * half + c, :, span(c, i)] = full.astype(BF16)
         for slot, to in enumerate(others):
             @pl.when(lax.rem(to, 2) == c)
             def _():
-                r_copy(slot, to).start()
+                r_piece(c, i, slot, to).start()
 
     for c in range(2):
-        for half in range(2):
-            A[half] = product(2 * half + c)
-
-        @pl.loop(0, nz)
-        def _(i):
-            at = rows_at(i, group)
-            both = jnp.concatenate([A[0, at], A[1, at]], 0)
-            S1[c, rows_at(i, m2)] = both.astype(BF16)
-
-        if c == 0:
-            go_along(0)
-        else:
-            go_near(1, S1[1])
+        for i in range(2):
+            for half in range(2):
+                A[half, :, span(c, i)] = product(2 * half + c, spans[c][i])
+
+            @pl.loop(0, nz)
+            def _(k):
+                at = rows_at(k, group)
+                both = jnp.concatenate([A[0, at, span(c, i)], A[1, at, span(c, i)]], 0)
+                S1[c, rows_at(k, m2), span(c, i)] = both.astype(BF16)
+
+            if c == 0:
+                go_along(0, i)
+    go_near(1, S1[1])
     get_near(q2_copy, 1)
     S1[1] = mix(to_z_ref[...], Q2[1])
-    go_along(1)
-    get_along(q1_copy, 0)
+    for i in range(2):
+        go_along(1, i)
+    for i in range(2):
+        get_along(q1_piece(0, i), 0)
     go_near(0, Q1[0])
     get_near(q2_copy, 0)
-    combine(0, Q2[0])
-    get_along(q1_copy, 1)
-    combine(1, Q1[1])
-
-    total = PTF[y]
+    for i in range(2):
+        combine(0, i, Q2[0, :, span(0, i)])
+    for i in range(2):
+        get_along(q1_piece(1, i), 1)
+        combine(1, i, Q1[1, :, span(1, i)])
+
+    for c in range(2):
+        @pl.when(odd == c)
+        def _():
+            for i in range(2):
+                total = PTF[y, :, span(c, i)]
+                for slot, to in enumerate(others):
+                    r_got = r_piece(c, i, slot, y)
+                    r_got.wait_recv()
+                    total = total + RS[slot, :, span(c, i)].astype(F32)
+                out_ref[:, span(c, i)] = total.astype(BF16)
+
     for slot, to in enumerate(others):
-        r_copy(slot, to).wait_recv()
-        total = total + RS[slot].astype(F32)
-    out_ref[...] = total.astype(BF16)
-
-    for slot, to in enumerate(others):
-        r_copy(slot, to).wait_send()
+        for c in range(2):
+            @pl.when(lax.rem(to, 2) == c)
+            def _():
+                for i in range(2):
+                    r_piece(c, i, slot, to).wait_send()
+
     for slot in (1, 2):
         for kind in range(2):
             t_own(slot, kind).wait_send()
@@ -476,7 +504,8 @@
     for j in range(4):
         sent_along(s2_copy, j)
     for c in range(2):
-        sent_along(q1_copy, c)
+        for i in range(2):
+            sent_along(q1_piece(c, i), c)
         sent_near(q2_copy, c)
 
 
@@ -494,7 +523,7 @@
     return pl.pallas_call(
         functools.partial(kernel, (nz, nd, share, parts)),
         out_shape=jax.ShapeDtypeStruct((toks, qw), BF16),
-        in_specs=[hbm] * 5 + [vmem] * 10,
+        in_specs=[hbm] * 5 + [vmem] * 5 + [hbm] * 2 + [vmem] * 2,
         out_specs=vmem,
         scratch_shapes=[
             pltpu.VMEM((4, 2 * toks, qw), BF16),
@@ -518,22 +547,24 @@
             pltpu.VMEM((rows, 2 * toks), BF16),
             pltpu.VMEM((rows, 2 * toks), BF16),
             pltpu.VMEM((2, 4 * toks, rows), BF16),
-            dma((5,)),
+            pltpu.VMEM((rows, rows), BF16),
+            pltpu.VMEM((rows, rows), BF16),
+            dma((7,)),
             dma((4, 2)), dma((4, 2)),
             dma((6, 2, 2)), dma((4, 2, 2)),
             dma((4,)), dma((4,)),
             dma((4, nd)), dma((4, nd)),
             dma((4, nz)), dma((4, nz)),
-            dma((2, nz)), dma((2, nz)),
+            dma((2, 2, nz)), dma((2, 2, nz)),
             dma((2, nd)), dma((2, nd)),
-            dma((3,)), dma((3,)),
+            dma((3, 2)), dma((3, 2)),
         ],
         compiler_params=pltpu.CompilerParams(
             collective_id=0, has_side_effects=True, vmem_limit_bytes=62 * 2**20
         ),
     )(
         tokens, tangents, gate_weight, up_weight, down_weight,
-        routes, routes.T, gates, readout.reshape(1, depth),
+        routes.T, gates.T, readout,
         jnp.asarray(expand, BF16), jnp.asarray(target, F32), jnp.asarray(to_z, BF16),
         jnp.asarray(to_d, BF16), jnp.asarray(expand_back, BF16), jnp.asarray(target_back, F32),
     )

time: 194 us -> 183 us (0.943); the launches traced: 193 us -> 180 us
  Pallas kernels: 188 us -> 178 us
  local copies, waits for them, and re-layouts: 5.78 us -> 1.65 us
    pallas_call x1, Pallas kernels: 188 us -> 178 us  [shards(): pl.pallas_call(functools.partial(kernel, (nz, nd, share, parts)), out_sha...]
    unnamed x3 -> x1, local copies, waits for them, and re-layouts: 4.47 us -> 1.65 us
where the time goes in v4:
time: 183 us; the launch traced here: 180 us
  Pallas kernels  178 us (97%)
    pallas_call x1, Pallas kernels, shards(): pl.pallas_call(functools.partial(kernel, (nz, nd, share, parts)), out_sha...  178 us

profile of v4, /device:TPU:9, one launch (start us, length us, event | category | flops | bytes accessed | tf_op | source)
XLA Modules:
  0.0 180.0 jit_solution(5327299754609032804)
XLA Ops:
  0.0 178.3 %shard_map.136 = bf16[128,896]{1,0:T(8,128)(2,1)} custom-call(bf16[128,896]{1,0:T(8,128)(2,1)} %tok_ref.1, bf16[128,896]{1,0:T(8,128)(2,1)} %tan_ref.1, bf16[1,3584,256]{2,1,0:T(8,128)(2,1)} %gw_ref.1, bf16[1,3584,256]{2,1,0:T(8,128)(2,1)} %uw_ref.1, bf16[1,256,3584]{2,1,0:T(8,128)(2,1)} %dw_ref.1, s32[8,128]{1,0:T(8,128)} %bitcast.2, f32[8,128]{1,0:T(8,128)} %bitcast.3, ...), custom_call_target="tpu_custom_call" | custom-call | tf_op jit(solution)/shard_map/pallas_call | solution.py:523
  178.3 1.6 copy.16

commit v5 on v4

--- a/solution.py
+++ b/solution.py
@@ -172,14 +172,14 @@
     def s1_copy(j, to, slot):
         at = rows_at(slot, m1)
         return remote(
-            S1.at[j, rows_at(to, m1)], R1.at[j, at] if j else X0.at[at],
+            S1.at[j, rows_at(to, m1)], R1.at[j, at] if j > 1 else X0.at[j, at],
             s1_send.at[j, to], s1_recv.at[j, slot], near(to),
         )
 
     def s2_copy(j, to, slot):
         at = rows_at(slot, m2)
         return remote(
-            S2.at[j, rows_at(to, m2)], R2.at[at, cols_of(j)] if j else R1.at[0, at],
+            S2.at[j, rows_at(to, m2)], R2.at[at, cols_of(j)] if j > 1 else R1.at[j, at],
             s2_send.at[j, to], s2_recv.at[j, slot], along(to),
         )
 
@@ -223,6 +223,23 @@
         send_near(s1_copy, j)
         R1[j, rows_at(d, m1)] = S1[j, rows_at(d, m1)]
 
+    def first(j):
+        S2[j] = mix(PZ[...], T[j])
+
+    def leave(j):
+        send_along(s2_copy, j)
+        R1[j, rows_at(z, m2)] = S2[j, rows_at(z, m2)]
+
+    def flip(j):
+        get_along(s2_copy, j)
+        S1[j] = mix(to_d_ref[...], R1[j])
+        send_near(s1_copy, j)
+        X0[j, rows_at(d, m1)] = S1[j, rows_at(d, m1)]
+
+    def finish(j):
+        get_near(s1_copy, j)
+        R2[:, cols_of(j)] = mix(to_z_ref[...], X0[j])
+
     def turn(j):
         get_near(s1_copy, j)
         S2[j] = mix(to_z_ref[...], R1[j])
@@ -231,9 +248,9 @@
 
     local[0].wait()
     local[1].wait()
-    S2[0] = mix(PZ[...], T[0])
+    first(0)
     pl.semaphore_wait(barrier, 2 * 3 + nd - 1 + nz - 1)
-    send_along(s2_copy, 0)
+    leave(0)
     for slot in (1, 2):
         for kind in range(2):
             t_own(slot, kind).start()
@@ -250,7 +267,6 @@
         for half, mat in pieces:
             w_from(2, half, mat, outer, half, 0).start()
 
-    R1[0, rows_at(z, m2)] = S2[0, rows_at(z, m2)]
     local[3].wait()
     local[4].wait()
     PD[...] = mix(to_d_ref[...], PZ[...])
@@ -282,22 +298,20 @@
     for kind in range(2):
         t_own(1, kind).wait_recv()
     t_on().start()
-    pack(1)
+    first(1)
+    leave(1)
     for kind in range(2):
         t_own(2, kind).wait_recv()
-    turn(1)
     pack(2)
+    flip(0)
+    turn(2)
     pass_on(2, 0)
     t_on().wait_recv()
     pack(3)
-    turn(2)
     pass_on(2, 1)
     pass_on(1, 0)
-    get_along(s2_copy, 0)
-    S1[0] = mix(to_d_ref[...], R1[0])
-    send_near(s1_copy, 0)
-    X0[rows_at(d, m1)] = S1[0, rows_at(d, m1)]
     turn(3)
+    flip(1)
     pass_on(1, 1)
 
     gate = jnp.zeros((experts, toks), F32)
@@ -316,8 +330,7 @@
         CB[0, pl.ds((2 * half + 1) * toks, toks)] = jnp.where(hit, low, 0.0).astype(BF16)
     CB[1] = mix(CB[0], to_d_ref[...])
 
-    get_near(s1_copy, 0)
-    R2[:, cols_of(0)] = mix(to_z_ref[...], X0[...])
+    finish(0)
 
     pass_on(3, 0)
     pass_on(3, 1)
@@ -339,8 +352,10 @@
         b_copy(slot, 0, y, 1 - core).wait_recv()
 
     for j in range(4):
-        if j:
+        if j > 1:
             get_along(s2_copy, j)
+        elif j == 1:
+            finish(1)
         cols = cols_of(j)
         for slot in range(4):
             H[slot] = (H[slot] if j else 0.0) + jnp.dot(R2[:, cols], W[slot, cols], preferred_element_type=F32)
@@ -543,7 +558,7 @@
             pltpu.VMEM((4, toks, qw), F32),
             pltpu.VMEM((4, toks, qw), BF16),
             pltpu.VMEM((3, toks, qw), BF16),
-            pltpu.VMEM((rows, qw), BF16),
+            pltpu.VMEM((2, rows, qw), BF16),
             pltpu.VMEM((rows, 2 * toks), BF16),
             pltpu.VMEM((rows, 2 * toks), BF16),
             pltpu.VMEM((2, 4 * toks, rows), BF16),

time: 183 us -> 180 us (0.984); the launches traced: 180 us -> 179 us
  no operation moved by 1% of the time
where the time goes in v5:
time: 180 us; the launch traced here: 179 us
  Pallas kernels  177 us (98%)
    pallas_call x1, Pallas kernels, shards(): pl.pallas_call(functools.partial(kernel, (nz, nd, share, parts)), out_sha...  177 us

profile of v5, /device:TPU:9, one launch (start us, length us, event | category | flops | bytes accessed | tf_op | source)
XLA Modules:
  0.0 179.1 jit_solution(3010077271811699567)
XLA Ops:
  0.0 177.5 %shard_map.136 = bf16[128,896]{1,0:T(8,128)(2,1)} custom-call(bf16[128,896]{1,0:T(8,128)(2,1)} %tok_ref.1, bf16[128,896]{1,0:T(8,128)(2,1)} %tan_ref.1, bf16[1,3584,256]{2,1,0:T(8,128)(2,1)} %gw_ref.1, bf16[1,3584,256]{2,1,0:T(8,128)(2,1)} %uw_ref.1, bf16[1,256,3584]{2,1,0:T(8,128)(2,1)} %dw_ref.1, s32[8,128]{1,0:T(8,128)} %bitcast.2, f32[8,128]{1,0:T(8,128)} %bitcast.3, ...), custom_call_target="tpu_custom_call" | custom-call | tf_op jit(solution)/shard_map/pallas_call | solution.py:538
  177.5 1.6 copy.16
